TPU v7x, 128 devices: a whole 4x4x4 slice. The times are simulated.
128 devices in a mesh: rep: 8 (over x, core), shard: 16 (over z, y).
Axes of the slice: x: 4, y: 4, z: 4, core: 2. Of those that a mesh axis runs over, the one named last changes fastest.
Arguments:
- tokens: bfloat16 [16384, 768], P(('rep', 'shard')), may hold values from -6 to 6
- segments: int32 [16384], P(('rep', 'shard')), may hold values from 0 to 23, as said below
- w_qkv: bfloat16 [768, 2304], P('shard'), may hold values from -0.21875 to 0.21875
- w_out: bfloat16 [768, 768], P('shard'), may hold values from -0.875 to 0.875
- w_up: bfloat16 [768, 3072], P('shard'), may hold values from -0.21875 to 0.21875
- w_down: bfloat16 [3072, 768], P('shard'), may hold values from -0.109375 to 0.109375
- b_query: bfloat16 [768], P('shard'), may hold values from -3 to 3
- b_value: bfloat16 [768], P('shard'), may hold values from -3 to 3
- b_out: bfloat16 [768], P('shard'), may hold values from -3 to 3
- b_up: bfloat16 [3072], P('shard'), may hold values from -3 to 3
- b_down: bfloat16 [768], P('shard'), may hold values from -3 to 3
- ln1_gain: bfloat16 [768], P('shard'), may hold values from 0.5 to 1.5
- ln1_shift: bfloat16 [768], P('shard'), may hold values from -2 to 2
- ln2_gain: bfloat16 [768], P('shard'), may hold values from 0.5 to 1.5
- ln2_shift: bfloat16 [768], P('shard'), may hold values from -2 to 2
- cotangent: bfloat16 [16384, 768], P(('rep', 'shard')), may hold values from -6 to 6
Outputs:
- out_tokens: bfloat16 [16384, 768], P(('rep', 'shard'))
- d_tokens: bfloat16 [16384, 768], P(('rep', 'shard'))
- d_w_qkv: float32 [768, 2304], P('shard')
- d_w_out: float32 [768, 768], P('shard')
- d_w_up: float32 [768, 3072], P('shard')
- d_w_down: float32 [3072, 768], P('shard')
- d_b_query: float32 [768], P('shard')
- d_b_value: float32 [768], P('shard')
- d_b_out: float32 [768], P('shard')
- d_b_up: float32 [3072], P('shard')
- d_b_down: float32 [768], P('shard')
- d_ln1_gain: float32 [768], P('shard')
- d_ln1_shift: float32 [768], P('shard')
- d_ln2_gain: float32 [768], P('shard')
- d_ln2_shift: float32 [768], P('shard')
Inputs may be any that keep to these rules, and one draw needn't show every extreme that they name: `segments`: numbers never fall along the tokens. The 2048 tokens of replica group r carry the numbers 3 r, 3 r + 1 and 3 r + 2; the middle document starts on a token of the group's first 128 and ends on one of its last 128, and the other two are shorter than 128 tokens.
All inputs are finite; a program needn't handle non-finite values.
Results may differ from a plain program's by a relative error of at most 0.024.
Values may be sent and summed in bfloat16 or wider, within the bound.
No kernel may reach another device: no remote copies, remote signals or barrier semaphores. Data moves between devices by JAX's collectives and lax.ppermute only.
A program may use at most 128 MiB of HBM per device.

v0:
```python
import jax
import jax.numpy as jnp
from jax import lax
from jax.sharding import PartitionSpec as P

HD = 64


def layer_norm(values, gain_vec, shift_vec):
    average = jnp.mean(values, axis=-1, keepdims=True)
    centered = values - average
    variance = jnp.mean(centered * centered, axis=-1, keepdims=True)
    return centered * lax.rsqrt(variance + 1e-05) * gain_vec + shift_vec


def body(
    tokens,
    segments,
    w_qkv,
    w_out,
    w_up,
    w_down,
    b_query,
    b_value,
    b_out,
    b_up,
    b_down,
    ln1_gain,
    ln1_shift,
    ln2_gain,
    ln2_shift,
    cotangent,
):
    row_count, model_width = tokens.shape
    head_count = model_width // HD
    score_scale = HD ** (-0.5)
    full_params = (
        lax.all_gather(w_qkv, "shard", axis=0, tiled=True),
        lax.all_gather(w_out, "shard", axis=0, tiled=True),
        lax.all_gather(w_up, "shard", axis=0, tiled=True),
        lax.all_gather(w_down, "shard", axis=0, tiled=True),
        lax.all_gather(b_query, "shard", axis=0, tiled=True),
        lax.all_gather(b_value, "shard", axis=0, tiled=True),
        lax.all_gather(b_out, "shard", axis=0, tiled=True),
        lax.all_gather(b_up, "shard", axis=0, tiled=True),
        lax.all_gather(b_down, "shard", axis=0, tiled=True),
        lax.all_gather(ln1_gain, "shard", axis=0, tiled=True),
        lax.all_gather(ln1_shift, "shard", axis=0, tiled=True),
        lax.all_gather(ln2_gain, "shard", axis=0, tiled=True),
        lax.all_gather(ln2_shift, "shard", axis=0, tiled=True),
    )
    qkv_full, out_full, up_full, down_full = (
        full_params[0],
        full_params[1],
        full_params[2],
        full_params[3],
    )
    bias_query = full_params[4].astype(jnp.float32)
    bias_value = full_params[5].astype(jnp.float32)
    bias_out = full_params[6].astype(jnp.float32)
    bias_up = full_params[7].astype(jnp.float32)
    bias_down = full_params[8].astype(jnp.float32)
    gain_one = full_params[9].astype(jnp.float32)
    shift_one = full_params[10].astype(jnp.float32)
    gain_two = full_params[11].astype(jnp.float32)
    shift_two = full_params[12].astype(jnp.float32)
    inputs = tokens.astype(jnp.float32)
    normed_one = layer_norm(inputs, gain_one, shift_one).astype(jnp.bfloat16)
    bias_cat = jnp.concatenate([bias_query, jnp.zeros_like(bias_query), bias_value])
    qkv_low = (jnp.dot(normed_one, qkv_full, preferred_element_type=jnp.float32) + bias_cat).astype(
        jnp.bfloat16
    )
    queries = qkv_low[:, :model_width]
    keys_low = qkv_low[:, model_width : 2 * model_width]
    values_low = qkv_low[:, 2 * model_width :]
    query_heads = queries.reshape(row_count, head_count, HD)
    first_pos = lax.axis_index("shard") * row_count
    last_pos = first_pos + row_count - 1
    query_pos = first_pos + jnp.arange(row_count, dtype=jnp.int32)

    def masked_scores(key_heads, seg_block, key_start):
        scores = (
            jnp.einsum("qhd,khd->hqk", query_heads, key_heads, preferred_element_type=jnp.float32)
            * score_scale
        )
        key_pos = key_start + jnp.arange(key_heads.shape[0], dtype=jnp.int32)
        allowed = (key_pos[None, :] <= query_pos[:, None]) & (
            seg_block[None, :] == segments[:, None]
        )
        return (jnp.where(allowed[None], scores, -1e30), allowed)

    def online_work(state_now, key_block, value_block, seg_block, key_start):
        row_max, denom_sum, accumulated = state_now
        piece_rows = key_block.shape[0]
        key_heads = key_block.reshape(piece_rows, head_count, HD)
        value_heads = value_block.reshape(piece_rows, head_count, HD)
        scores, allowed = masked_scores(key_heads, seg_block, key_start)
        new_max = jnp.maximum(row_max, jnp.max(scores, axis=-1))
        weights = jnp.where(allowed[None], jnp.exp(scores - new_max[:, :, None]), 0.0)
        factor = jnp.exp(row_max - new_max)
        denom_sum = denom_sum * factor + jnp.sum(weights, axis=-1)
        accumulated = accumulated * factor.T[:, :, None] + jnp.einsum(
            "hqk,khd->qhd",
            weights.astype(jnp.bfloat16),
            value_heads,
            preferred_element_type=jnp.float32,
        )
        return (new_max, denom_sum, accumulated)

    def online_step(state_now, key_block, value_block, seg_block, key_start):
        return lax.cond(
            key_start <= last_pos,
            lambda held: online_work(held, key_block, value_block, seg_block, key_start),
            lambda held: held,
            state_now,
        )

    start_state = (
        jnp.full((head_count, row_count), -1e30, jnp.float32),
        jnp.zeros((head_count, row_count), jnp.float32),
        jnp.zeros((row_count, head_count, HD), jnp.float32),
    )
    state_now = start_state
    key_piece = lax.all_gather(keys_low, "shard", axis=0, tiled=True)
    value_piece = lax.all_gather(values_low, "shard", axis=0, tiled=True)
    seg_piece = lax.all_gather(segments, "shard", axis=0, tiled=True)
    piece_rows = key_piece.shape[0]

    def inner_step(state_in, block_index):
        offset = block_index * 512
        key_block = lax.dynamic_slice_in_dim(key_piece, offset, 512, 0)
        value_block = lax.dynamic_slice_in_dim(value_piece, offset, 512, 0)
        seg_block = lax.dynamic_slice_in_dim(seg_piece, offset, 512, 0)
        return (online_step(state_in, key_block, value_block, seg_block, offset), None)

    state_now, _ = lax.scan(inner_step, state_now, jnp.arange(piece_rows // 512, dtype=jnp.int32))
    row_max, denom_sum, accumulated = state_now
    attended_heads = accumulated / denom_sum.T[:, :, None]
    log_total = row_max + jnp.log(denom_sum)
    attended_low = attended_heads.reshape(row_count, model_width).astype(jnp.bfloat16)
    middle = inputs + jnp.dot(attended_low, out_full, preferred_element_type=jnp.float32) + bias_out
    normed_two = layer_norm(middle, gain_two, shift_two).astype(jnp.bfloat16)
    upward = jnp.dot(normed_two, up_full, preferred_element_type=jnp.float32) + bias_up
    activated, gelu_pull = jax.vjp(jax.nn.gelu, upward)
    activated_low = activated.astype(jnp.bfloat16)
    result = (
        middle + jnp.dot(activated_low, down_full, preferred_element_type=jnp.float32) + bias_down
    )
    out_tokens = result.astype(jnp.bfloat16)
    back_params = (
        lax.all_gather(w_qkv, "shard", axis=0, tiled=True),
        lax.all_gather(w_out, "shard", axis=0, tiled=True),
        lax.all_gather(w_up, "shard", axis=0, tiled=True),
        lax.all_gather(w_down, "shard", axis=0, tiled=True),
        lax.all_gather(b_query, "shard", axis=0, tiled=True),
        lax.all_gather(b_value, "shard", axis=0, tiled=True),
        lax.all_gather(b_out, "shard", axis=0, tiled=True),
        lax.all_gather(b_up, "shard", axis=0, tiled=True),
        lax.all_gather(b_down, "shard", axis=0, tiled=True),
        lax.all_gather(ln1_gain, "shard", axis=0, tiled=True),
        lax.all_gather(ln1_shift, "shard", axis=0, tiled=True),
        lax.all_gather(ln2_gain, "shard", axis=0, tiled=True),
        lax.all_gather(ln2_shift, "shard", axis=0, tiled=True),
    )
    qkv_back, out_back, up_back, down_back = (
        back_params[0],
        back_params[1],
        back_params[2],
        back_params[3],
    )
    gain_one_back = back_params[9].astype(jnp.float32)
    shift_one_back = back_params[10].astype(jnp.float32)
    gain_two_back = back_params[11].astype(jnp.float32)
    shift_two_back = back_params[12].astype(jnp.float32)
    grad_float = cotangent.astype(jnp.float32)
    d_down = jnp.einsum("tf,td->fd", activated_low, cotangent, preferred_element_type=jnp.float32)
    d_bias_down = jnp.sum(grad_float, axis=0)
    d_activated = jnp.einsum("td,fd->tf", cotangent, down_back, preferred_element_type=jnp.float32)
    (d_upward,) = gelu_pull(d_activated)
    d_up_low = d_upward.astype(jnp.bfloat16)
    d_up = jnp.einsum("td,tf->df", normed_two, d_up_low, preferred_element_type=jnp.float32)
    d_bias_up = jnp.sum(d_up_low.astype(jnp.float32), axis=0)
    d_normed_two = jnp.einsum("tf,df->td", d_up_low, up_back, preferred_element_type=jnp.float32)
    _, norm_two_pull = jax.vjp(layer_norm, middle, gain_two_back, shift_two_back)
    d_mid_norm, d_gain_two, d_shift_two = norm_two_pull(d_normed_two)
    d_middle = grad_float + d_mid_norm
    d_branch = d_middle.astype(jnp.bfloat16)
    d_out = jnp.einsum("td,te->de", attended_low, d_branch, preferred_element_type=jnp.float32)
    d_bias_out = jnp.sum(d_branch.astype(jnp.float32), axis=0)
    d_attended = jnp.einsum(
        "te,de->td", d_branch, out_back, preferred_element_type=jnp.float32
    ).astype(jnp.bfloat16)
    dout_heads = d_attended.reshape(row_count, head_count, HD)
    row_delta = jnp.sum(dout_heads.astype(jnp.float32) * attended_heads, axis=-1).T
    all_keys, all_values, all_segs = (
        lax.all_gather(keys_low, "shard", axis=0, tiled=True),
        lax.all_gather(values_low, "shard", axis=0, tiled=True),
        lax.all_gather(segments, "shard", axis=0, tiled=True),
    )
    key_count = all_keys.shape[0]
    block_rows = min(512, key_count)
    pair_zero = jnp.zeros((block_rows, 2 * model_width), jnp.float32)
    dq_zero = jnp.zeros((row_count, head_count, HD), jnp.float32)

    def back_work(offset):
        key_block = lax.dynamic_slice_in_dim(all_keys, offset, block_rows, 0).reshape(
            block_rows, head_count, HD
        )
        value_block = lax.dynamic_slice_in_dim(all_values, offset, block_rows, 0).reshape(
            block_rows, head_count, HD
        )
        seg_block = lax.dynamic_slice_in_dim(all_segs, offset, block_rows, 0)
        scores, allowed = masked_scores(key_block, seg_block, offset)
        soft_weights = jnp.where(allowed[None], jnp.exp(scores - log_total[:, :, None]), 0.0)
        d_probs = jnp.einsum(
            "qhd,khd->hqk", dout_heads, value_block, preferred_element_type=jnp.float32
        )
        d_scores = (soft_weights * (d_probs - row_delta[:, :, None])).astype(jnp.bfloat16)
        dq_add = (
            jnp.einsum("hqk,khd->qhd", d_scores, key_block, preferred_element_type=jnp.float32)
            * score_scale
        )
        d_values = jnp.einsum(
            "hqk,qhd->khd",
            soft_weights.astype(jnp.bfloat16),
            dout_heads,
            preferred_element_type=jnp.float32,
        )
        d_keys = (
            jnp.einsum("hqk,qhd->khd", d_scores, query_heads, preferred_element_type=jnp.float32)
            * score_scale
        )
        return (
            dq_add,
            jnp.concatenate(
                [
                    d_keys.reshape(block_rows, model_width),
                    d_values.reshape(block_rows, model_width),
                ],
                axis=-1,
            ),
        )

    block_list = jnp.arange(key_count // block_rows, dtype=jnp.int32)

    def back_step(dq_state, block_index):
        offset = block_index * block_rows
        dq_add, pair_rows = lax.cond(
            offset <= last_pos,
            lambda held: back_work(held),
            lambda held: (dq_zero, pair_zero),
            offset,
        )
        return (dq_state + dq_add, pair_rows)

    dq_sum, key_pieces = lax.scan(back_step, dq_zero, block_list)
    key_terms = key_pieces.reshape(key_count, 2 * model_width)
    key_value_grad = lax.psum_scatter(
        key_terms.astype(jnp.bfloat16), "shard", scatter_dimension=0, tiled=True
    )
    d_qkv = jnp.concatenate(
        [dq_sum.reshape(row_count, model_width).astype(jnp.bfloat16), key_value_grad], axis=-1
    )
    d_qkv_w = jnp.einsum("td,te->de", normed_one, d_qkv, preferred_element_type=jnp.float32)
    d_bias_query = jnp.sum(d_qkv[:, :model_width].astype(jnp.float32), axis=0)
    d_bias_value = jnp.sum(d_qkv[:, 2 * model_width :].astype(jnp.float32), axis=0)
    d_normed_one = jnp.einsum("te,de->td", d_qkv, qkv_back, preferred_element_type=jnp.float32)
    _, norm_one_pull = jax.vjp(layer_norm, inputs, gain_one_back, shift_one_back)
    d_in_norm, d_gain_one, d_shift_one = norm_one_pull(d_normed_one)
    d_tokens = (d_middle + d_in_norm).astype(jnp.bfloat16)
    shares = (
        lax.psum_scatter(
            d_qkv_w.astype(jnp.bfloat16), "shard", scatter_dimension=0, tiled=True
        ).astype(jnp.float32),
        lax.psum_scatter(
            d_out.astype(jnp.bfloat16), "shard", scatter_dimension=0, tiled=True
        ).astype(jnp.float32),
        lax.psum_scatter(
            d_up.astype(jnp.bfloat16), "shard", scatter_dimension=0, tiled=True
        ).astype(jnp.float32),
        lax.psum_scatter(
            d_down.astype(jnp.bfloat16), "shard", scatter_dimension=0, tiled=True
        ).astype(jnp.float32),
        lax.psum_scatter(
            d_bias_query.astype(jnp.bfloat16), "shard", scatter_dimension=0, tiled=True
        ).astype(jnp.float32),
        lax.psum_scatter(
            d_bias_value.astype(jnp.bfloat16), "shard", scatter_dimension=0, tiled=True
        ).astype(jnp.float32),
        lax.psum_scatter(
            d_bias_out.astype(jnp.bfloat16), "shard", scatter_dimension=0, tiled=True
        ).astype(jnp.float32),
        lax.psum_scatter(
            d_bias_up.astype(jnp.bfloat16), "shard", scatter_dimension=0, tiled=True
        ).astype(jnp.float32),
        lax.psum_scatter(
            d_bias_down.astype(jnp.bfloat16), "shard", scatter_dimension=0, tiled=True
        ).astype(jnp.float32),
        lax.psum_scatter(
            d_gain_one.astype(jnp.bfloat16), "shard", scatter_dimension=0, tiled=True
        ).astype(jnp.float32),
        lax.psum_scatter(
            d_shift_one.astype(jnp.bfloat16), "shard", scatter_dimension=0, tiled=True
        ).astype(jnp.float32),
        lax.psum_scatter(
            d_gain_two.astype(jnp.bfloat16), "shard", scatter_dimension=0, tiled=True
        ).astype(jnp.float32),
        lax.psum_scatter(
            d_shift_two.astype(jnp.bfloat16), "shard", scatter_dimension=0, tiled=True
        ).astype(jnp.float32),
    )
    summed = (
        lax.psum(shares[0].astype(jnp.bfloat16), "rep").astype(jnp.float32),
        lax.psum(shares[1].astype(jnp.bfloat16), "rep").astype(jnp.float32),
        lax.psum(shares[2].astype(jnp.bfloat16), "rep").astype(jnp.float32),
        lax.psum(shares[3].astype(jnp.bfloat16), "rep").astype(jnp.float32),
        lax.psum(shares[4].astype(jnp.bfloat16), "rep").astype(jnp.float32),
        lax.psum(shares[5].astype(jnp.bfloat16), "rep").astype(jnp.float32),
        lax.psum(shares[6].astype(jnp.bfloat16), "rep").astype(jnp.float32),
        lax.psum(shares[7].astype(jnp.bfloat16), "rep").astype(jnp.float32),
        lax.psum(shares[8].astype(jnp.bfloat16), "rep").astype(jnp.float32),
        lax.psum(shares[9].astype(jnp.bfloat16), "rep").astype(jnp.float32),
        lax.psum(shares[10].astype(jnp.bfloat16), "rep").astype(jnp.float32),
        lax.psum(shares[11].astype(jnp.bfloat16), "rep").astype(jnp.float32),
        lax.psum(shares[12].astype(jnp.bfloat16), "rep").astype(jnp.float32),
    )
    return (
        out_tokens,
        d_tokens,
        summed[0],
        summed[1],
        summed[2],
        summed[3],
        summed[4],
        summed[5],
        summed[6],
        summed[7],
        summed[8],
        summed[9],
        summed[10],
        summed[11],
        summed[12],
    )


def solution(mesh):
    placed = (
        P(("rep", "shard"), None),
        P(("rep", "shard")),
        P("shard", None),
        P("shard", None),
        P("shard", None),
        P("shard", None),
        P("shard"),
        P("shard"),
        P("shard"),
        P("shard"),
        P("shard"),
        P("shard"),
        P("shard"),
        P("shard"),
        P("shard"),
        P(("rep", "shard"), None),
    )
    return jax.shard_map(
        body,
        mesh=mesh,
        in_specs=placed,
        out_specs=(
            P(("rep", "shard"), None),
            P(("rep", "shard"), None),
            P("shard", None),
            P("shard", None),
            P("shard", None),
            P("shard", None),
            P("shard"),
            P("shard"),
            P("shard"),
            P("shard"),
            P("shard"),
            P("shard"),
            P("shard"),
            P("shard"),
            P("shard"),
        ),
        check_vma=False,
    )
```

profile of v0, /device:TPU:1, one launch (start us, length us, event | category | flops | bytes accessed | tf_op | source)
XLA Modules:
  0.0 862.5 jit_solution(16119801090116370511)
XLA Ops:
  18.1 63.0 %all-reduce.19 = (bf16[768]{0:T(1024)(128)(2,1)S(1)}, bf16[768]{0:T(1024)(128)(2,1)S(1)}, bf16[768]{0:T(1024)(128)(2,1)S(1)}, bf16[768]{0:T(1024)(128)(2,1)S(1)}...) all-reduce(bf16[768]{0:T(1024)(128)(2,1)S(1)} %dynamic-update-slice, ...), channel_id=1, replica_groups=mesh['rep'=8,'shard'=16] {'shard'}, use_global_device_ids=true, to_apply=%add.3 | all-reduce | flops 8448 | bytes 33792
  89.3 15.6 %all-gather = s32[16,1,128]{2,1,0:T(1,128)} all-gather(s32[1,1,128]{2,1,0:T(1,128)} %bitcast.15), channel_id=1, replica_groups=mesh['rep'=8,'shard'=16] {'shard'}, dimensions={0}, use_global_device_ids=true | all-gather | bytes 8704 | tf_op jit(solution)/shard_map/all_gather | solution.py:126
  105.1 13.2 %all-gather.18.cloned.1.call-done = bf16[3072,768]{1,0:T(8,128)(2,1)} async-done(((bf16[192,768]{1,0:T(8,128)(2,1)}), bf16[3072,768]{1,0:T(8,128)(2,1)}) %all-gather.18.cloned.1.call-update) | async-done | bytes 4718608 | tf_op jit(solution)/shard_map/all_gather | solution.py:41
  122.3 46.1 %all-gather.12.cloned.1.call-done = bf16[2048,768]{1,0:T(8,128)(2,1)} async-done(((bf16[128,768]{1,0:T(8,128)(2,1)}), bf16[2048,768]{1,0:T(8,128)(2,1)}) %all-gather.12.cloned.1.call-update) | async-done | bytes 3145744 | tf_op jit(solution)/shard_map/all_gather | solution.py:125
  168.4 4.7 copy.74
  173.1 44.8 %all-gather.10.cloned.1.call-done = bf16[2048,768]{1,0:T(8,128)(2,1)} async-done(((bf16[128,768]{1,0:T(8,128)(2,1)}), bf16[2048,768]{1,0:T(8,128)(2,1)}) %all-gather.10.cloned.1.call-update) | async-done | bytes 3145744 | tf_op jit(solution)/shard_map/all_gather | solution.py:124
  217.9 4.8 copy.73
  222.7 11.8 %while.28 = (s32[]{:T(128)}, f32[12,128]{1,0:T(8,128)S(1)}, f32[12,128]{1,0:T(8,128)S(1)}, f32[128,12,64]{0,2,1:T(8,128)S(1)}, s32[4]{0:T(128)S(1)}, /*index=5*/...) while((s32[]{:T(128)}, f32[12,128]{1,0:T(8,128)S(1)}, ...), condition=%wide.region_7.8_spmd.clone, body=%wide.region_2.7_spmd.clone.sunk | while | flops 211948672 | bytes 15512437 | solution.py:136
  223.9 6.7 conditional.6
  234.6 26.7 %all-gather.14.cloned.1.call-done = bf16[768,768]{1,0:T(8,128)(2,1)} async-done(((bf16[48,768]{1,0:T(8,128)(2,1)}), bf16[768,768]{1,0:T(8,128)(2,1)}) %all-gather.14.cloned.1.call-update) | async-done | bytes 1179664 | tf_op jit(solution)/shard_map/all_gather | solution.py:39
  263.9 53.7 %all-gather.16.cloned.1.call-done = bf16[768,3072]{1,0:T(8,128)(2,1)} async-done(((bf16[48,3072]{1,0:T(8,128)(2,1)}), bf16[768,3072]{1,0:T(8,128)(2,1)}) %all-gather.16.cloned.1.call-update) | async-done | bytes 4718608 | tf_op jit(solution)/shard_map/all_gather | solution.py:40
  317.6 6.2 fusion.69
  330.8 30.0 %while.29 = (s32[]{:T(128)}, f32[128,12,64]{0,2,1:T(8,128)}, bf16[4,512,1536]{2,1,0:T(8,128)(2,1)}, s32[4]{0:T(128)S(1)}, s32[]{:T(128)}, /*index=5*/bf16[2048,7...) while((s32[]{:T(128)}, f32[128,12,64]{0,2,1:T(8,128)}, ...), condition=%wide.region_16.17_spmd.clone, body=%wide.region_13.0_spmd.clone.sunk | while | flops 517177984 | bytes 33258536 | solution.py:256
  332.1 10.1 %conditional.7 = (f32[128,12,64]{0,2,1:T(8,128)S(1)}, bf16[1,512,1536]{1,2,0:T(8,128)(2,1)S(1)}) conditional(s32[]{:T(128)} %convert_element_type.327, () %tuple.106, (s32[]{:T(128)}, bf16[2048,768]{0,1:T(8,128)(2,1)}, s32[]{:T(128)}, s32[2048]{0:T(1024)}, s32[128]{0:T(128)}, /*index=5*/bf16[128,12,64]{0,2,1:T(8,128)(2,1)S(1)}, ...), branch_computations={%region_14.14_spmd, %region_15.15_spmd} | conditional | flops 516981376 | bytes 25786434 | solution.py:248
  373.8 96.6 %reduce-scatter.6.cloned.1.call-done = bf16[128,1536]{1,0:T(8,128)(2,1)} async-done(((bf16[2048,1536]{1,0:T(8,128)(2,1)}), bf16[128,1536]{1,0:T(8,128)(2,1)}) %reduce-scatter.6.cloned.1.call-update) | async-done | bytes 393232 | tf_op jit(solution)/shard_map/reduce_scatter | solution.py:258
  470.3 4.0 convolution_convert_fusion.2
  477.3 4.1 fusion.68
  481.7 58.1 %all-reduce.18 = (bf16[768]{0:T(1024)(128)(2,1)S(1)}, bf16[768]{0:T(1024)(128)(2,1)S(1)}, bf16[768]{0:T(1024)(128)(2,1)S(1)}, bf16[768]{0:T(1024)(128)(2,1)S(1)}...) all-reduce(bf16[768]{0:T(1024)(128)(2,1)} %copy-done.28, ...), channel_id=1, replica_groups=mesh['rep'=8,'shard'=16] {'shard'}, use_global_device_ids=true, to_apply=%add.8 | all-reduce | flops 9984 | bytes 39936
  540.5 28.3 %all-reduce.20 = (bf16[48]{0:T(256)(128)(2,1)S(1)}, bf16[48]{0:T(256)(128)(2,1)S(1)}, bf16[48]{0:T(256)(128)(2,1)S(1)}, bf16[192]{0:T(256)(128)(2,1)S(1)}, bf16[...) all-reduce(bf16[48]{0:T(256)(128)(2,1)S(1)} %dynamic-slice.10, ...), channel_id=1, replica_groups=mesh['rep'=8,'shard'=16] {'rep'}, use_global_device_ids=true, to_apply=%region_30.31 | all-reduce | flops 576 | bytes 2304 | tf_op jit(solution)/shard_map/psum | solution.py:317
  575.0 51.8 %reduce-scatter.12.cloned.1.call-done = bf16[48,3072]{1,0:T(8,128)(2,1)} async-done(((bf16[768,3072]{1,0:T(8,128)(2,1)}), bf16[48,3072]{1,0:T(8,128)(2,1)}) %reduce-scatter.12.cloned.1.call-update) | async-done | bytes 294928 | tf_op jit(solution)/shard_map/reduce_scatter | solution.py:278
  626.8 80.9 %reduce-scatter.14.cloned.1.call-done = bf16[192,768]{1,0:T(8,128)(2,1)} async-done(((bf16[3072,768]{1,0:T(8,128)(2,1)}), bf16[192,768]{1,0:T(8,128)(2,1)}) %reduce-scatter.14.cloned.1.call-update) | async-done | bytes 294928 | tf_op jit(solution)/shard_map/reduce_scatter | solution.py:281
  707.8 79.0 %reduce-scatter.8.cloned.1.call-done = bf16[48,2304]{1,0:T(8,128)(2,1)} async-done(((bf16[768,2304]{1,0:T(8,128)(2,1)}), bf16[48,2304]{1,0:T(8,128)(2,1)}) %reduce-scatter.8.cloned.1.call-update) | async-done | bytes 221200 | tf_op jit(solution)/shard_map/reduce_scatter | solution.py:272
  786.8 4.1 fusion.46
  790.9 58.7 %all-reduce.24.cloned.1.call-done = (bf16[48,2304]{1,0:T(8,128)(2,1)}, bf16[48,768]{1,0:T(8,128)(2,1)}, bf16[48,3072]{1,0:T(8,128)(2,1)}, bf16[192,768]{1,0:T(8,128)(2,1)}) async-done(((bf16[48,2304]{1,0:T(8,128)(2,1)}, bf16[48,768]{1,0:T(8,128)(2,1)}, bf16[48,3072]{1,0:T(8,128)(2,1)}, bf16[192,768]{1,0:T(8,128)(2,1)}), (bf16[48,2304]{1,0:T(8,128)(2,1)}, bf16[48,768]{1,0:T(8,128)(2,1)}, ...) | async-done | bytes 884752 | tf_op jit(solution)/shard_map/psum | solution.py:313
  (262 shorter events, 95.5 us)
Async XLA Ops:
  7.2 76.2 %all-gather.8.cloned.1.call-start = ((), (), s32[]{:S(2)}) async-start(), calls=%async_computation.5 | async-start | bytes 3760128 | tf_op jit(solution)/shard_map/all_gather | solution.py:38
  7.9 110.4 %all-gather.18.cloned.1.call-start = ((), (), s32[]{:S(2)}) async-start(), calls=%async_computation.10 | async-start | bytes 5013504 | tf_op jit(solution)/shard_map/all_gather | solution.py:41
  8.7 159.7 %all-gather.12.cloned.1.call-start = ((), (), s32[]{:S(2)}) async-start(), calls=%async_computation.7 | async-start | bytes 3342336 | tf_op jit(solution)/shard_map/all_gather | solution.py:125
  86.7 31.6 %copy-start.8 = (bf16[128,768]{1,0:T(8,128)(2,1)S(1)}, bf16[128,768]{1,0:T(8,128)(2,1)}, u32[]{:S(2)}) copy-start(bf16[128,768]{1,0:T(8,128)(2,1)} %param.39) | copy-start | bytes 589828
  87.5 130.4 %all-gather.10.cloned.1.call-start = ((), (), s32[]{:S(2)}) async-start(), calls=%async_computation.6 | async-start | bytes 3342336 | tf_op jit(solution)/shard_map/all_gather | solution.py:124
  88.1 173.2 %all-gather.14.cloned.1.call-start = ((), (), s32[]{:S(2)}) async-start(), calls=%async_computation.8 | async-start | bytes 1253376 | tf_op jit(solution)/shard_map/all_gather | solution.py:39
  88.7 228.9 %all-gather.16.cloned.1.call-start = ((), (), s32[]{:S(2)}) async-start(), calls=%async_computation.9 | async-start | bytes 5013504 | tf_op jit(solution)/shard_map/all_gather | solution.py:40
  89.2 381.1 %reduce-scatter.6.cloned.1.call-start = ((), (), s32[]{:S(2)}) async-start(), calls=%async_computation.11 | async-start | bytes 6684672 | tf_op jit(solution)/shard_map/reduce_scatter | solution.py:258
  222.7 38.7 %copy-start.2 = (bf16[128,768]{1,0:T(8,128)(2,1)S(1)}, bf16[128,768]{1,0:T(8,128)(2,1)}, u32[]{:S(2)}) copy-start(bf16[128,768]{1,0:T(8,128)(2,1)} %param.24) | copy-start | bytes 589828
  234.6 89.2 %copy-start.12 = (bf16[128,12,64]{0,2,1:T(8,128)(2,1)}, bf16[128,12,64]{0,2,1:T(8,128)(2,1)S(1)}, u32[]{:S(2)}) copy-start(bf16[128,12,64]{0,2,1:T(8,128)(2,1)S(1)} %fusion.60) | copy-start | bytes 589828
  263.0 63.1 %copy-start = (f32[128,768]{1,0:T(8,128)}, f32[128,768]{1,0:T(8,128)S(1)}, u32[]{:S(2)}) copy-start(f32[128,768]{1,0:T(8,128)S(1)} %get-tuple-element.621) | copy-start | bytes 1179652
  263.1 63.1 %copy-start.23 = (f32[128]{0:T(128)}, f32[128]{0:T(128)S(1)}, u32[]{:S(2)}) copy-start(f32[128]{0:T(128)S(1)} %broadcast_multiply_fusion) | copy-start | bytes 1540
  263.3 62.9 %copy-start.25 = (f32[128]{0:T(128)}, f32[128]{0:T(128)S(1)}, u32[]{:S(2)}) copy-start(f32[128]{0:T(128)S(1)} %fusion.62) | copy-start | bytes 1540
  317.6 6.2 copy-start.5
  360.9 214.1 %reduce-scatter.10.cloned.1.call-start = ((), (), s32[]{:S(2)}) async-start(), calls=%async_computation.13 | async-start | bytes 1253376 | tf_op jit(solution)/shard_map/reduce_scatter | solution.py:275
  363.4 263.5 %reduce-scatter.12.cloned.1.call-start = ((), (), s32[]{:S(2)}) async-start(), calls=%async_computation.14 | async-start | bytes 5013504 | tf_op jit(solution)/shard_map/reduce_scatter | solution.py:278
  367.2 340.6 %reduce-scatter.14.cloned.1.call-start = ((), (), s32[]{:S(2)}) async-start(), calls=%async_computation.15 | async-start | bytes 5013504 | tf_op jit(solution)/shard_map/reduce_scatter | solution.py:281
  372.4 98.0 %copy-start.20 = (f32[128]{0:T(128)S(1)}, f32[128]{0:T(128)}, u32[]{:S(2)}) copy-start(f32[128]{0:T(128)} %copy-done.19) | copy-start | bytes 1540
  372.4 98.0 %copy-start.22 = (f32[128]{0:T(128)S(1)}, f32[128]{0:T(128)}, u32[]{:S(2)}) copy-start(f32[128]{0:T(128)} %copy-done.21) | copy-start | bytes 1540
  372.4 414.4 %reduce-scatter.8.cloned.1.call-start = ((), (), s32[]{:S(2)}) async-start(), calls=%async_computation.12 | async-start | bytes 3760128 | tf_op jit(solution)/shard_map/reduce_scatter | solution.py:272
  373.8 100.5 %copy-start.17 = (bf16[128,768]{1,0:T(8,128)(2,1)}, bf16[128,768]{1,0:T(8,128)(2,1)S(1)}, u32[]{:S(2)}) copy-start(bf16[128,768]{1,0:T(8,128)(2,1)S(1)} %copy.79) | copy-start | bytes 589828
  474.3 375.3 %all-reduce.24.cloned.1.call-start = ((), (), s32[]{:S(2)}) async-start(), calls=%async_computation.16 | async-start | bytes 1769472 | tf_op jit(solution)/shard_map/psum | solution.py:313
  477.3 96.2 %copy-start.7 = (f32[128,768]{1,0:T(8,128)S(1)}, f32[128,768]{1,0:T(8,128)}, u32[]{:S(2)}) copy-start(f32[128,768]{1,0:T(8,128)} %copy-done.6) | copy-start | bytes 1179652
  849.6 5.1 copy-start.18
  (29 other events, 53.2 us)
Sparse Core Ops, SparseCore 0:
  10.1 52.5 all-gather.7
  64.8 53.4 all-gather.17
  121.0 47.3 all-gather.11
  170.9 46.8 all-gather.9
  219.8 41.4 all-gather.13
  263.3 54.2 all-gather.15
  361.0 109.3 reduce-scatter.5
  473.5 72.1 reduce-scatter.9
  549.1 77.6 reduce-scatter.11
  630.0 77.6 reduce-scatter.13
  711.2 75.6 reduce-scatter.7
  789.3 60.3 all-reduce.23
where the time goes:
time: 866 us; the launch traced here: 862 us
  waiting for transfers between devices  555 us (64%)
  blocking collectives  165 us (19%)
  matrix products  46.7 us (5%)
  local copies, waits for them, and re-layouts  43.8 us (5%)
  other arithmetic  28.7 us (3%)
  between operations  17.3 us (2%)
    unnamed x2, blocking collectives  121 us
    reduce_scatter x1, waiting for transfers between devices, body(): lax.psum_scatter(key_terms.astype(jnp.bfloat16), 'shard', scatter_dimensi...  96.6 us
    reduce_scatter x1, waiting for transfers between devices, body(): lax.psum_scatter(d_down.astype(jnp.bfloat16), 'shard', scatter_dimension=...  80.9 us
    reduce_scatter x1, waiting for transfers between devices, body(): lax.psum_scatter(d_qkv_w.astype(jnp.bfloat16), 'shard', scatter_dimension...  79 us
    psum x1, waiting for transfers between devices, body(): lax.psum(shares[0].astype(jnp.bfloat16), 'rep').astype(jnp.float32)  58.7 us
    all_gather x1, waiting for transfers between devices, body(): lax.all_gather(w_up, 'shard', axis=0, tiled=True)  53.7 us
    reduce_scatter x1, waiting for transfers between devices, body(): lax.psum_scatter(d_up.astype(jnp.bfloat16), 'shard', scatter_dimension=0,...  51.8 us
    all_gather x1, waiting for transfers between devices, body(): value_piece = lax.all_gather(values_low, 'shard', axis=0, tiled=True)  46.1 us
  transfers between devices with their start and end apart: 12, of which 10 were waited for; matrix products, arithmetic and copies ran while one was open for 8% of the time, Pallas kernels for 0%

commit v1 on v0

v1 whole, which is shorter than its diff:
```python
import jax
import jax.numpy as jnp
from jax import lax
from jax.experimental import pallas as pl
from jax.experimental.pallas import tpu as pltpu
from jax.sharding import Mesh, PartitionSpec as P

HD = 64
TOK = 128
D = 768
HEADS = 3
WIDTH = HEADS * HD
CHUNK = 512
LOW = jnp.bfloat16
WIDE = jnp.float32


def dot(left, right, dims=((1,), (0,))):
    return lax.dot_general(left, right, (dims, ((), ())), preferred_element_type=WIDE)


def masked(scores, start, place, chunk, block):
    if chunk != block and chunk != 0 and block != 3:
        return scores
    spots = lax.broadcasted_iota(jnp.int32, scores.shape, 0) + chunk * CHUNK
    allowed = None
    if chunk == 0 or block == 3:
        allowed = spots >= start
    if chunk == block:
        causal = spots <= place
        allowed = causal if allowed is None else allowed & causal
    return jnp.where(allowed, scores, -1e30)


def chunk_rows(kv_ref, chunk, low, high):
    return jnp.concatenate(
        [kv_ref[y, chunk * TOK : (chunk + 1) * TOK, low:high] for y in range(4)], axis=0
    )


def forward_kernel(q_ref, kv_ref, bound_ref, att_ref, lse_ref):
    for block in range(4):
        rows = slice(block * TOK, (block + 1) * TOK)
        start = bound_ref[0:1, rows]
        place = bound_ref[1:2, rows]
        for head in range(HEADS):
            cols = slice(head * HD, (head + 1) * HD)
            query = q_ref[rows, cols]
            scores = []
            for chunk in range(block + 1):
                keys = chunk_rows(kv_ref, chunk, head * HD, head * HD + HD)
                scores.append(
                    masked(dot(keys, query, ((1,), (1,))), start, place, chunk, block)
                )
            top = scores[0].max(axis=0, keepdims=True)
            for item in scores[1:]:
                top = jnp.maximum(top, item.max(axis=0, keepdims=True))
            total = jnp.zeros((1, TOK), WIDE)
            summed = jnp.zeros((HD, TOK), WIDE)
            for chunk in range(block + 1):
                weights = jnp.exp(scores[chunk] - top)
                total = total + weights.sum(axis=0, keepdims=True)
                values = chunk_rows(kv_ref, chunk, WIDTH + head * HD, WIDTH + head * HD + HD)
                summed = summed + dot(values, weights.astype(LOW), ((0,), (0,)))
            att_ref[rows, cols] = jnp.transpose(summed / total).astype(LOW)
            lse_ref[head : head + 1, rows] = top + jnp.log(total)


def backward_kernel(q_ref, kv_ref, bound_ref, lse_ref, do_ref, dq_ref, dkv_ref, p_ref, ds_ref):
    for head in range(HEADS):
        cols = slice(head * HD, (head + 1) * HD)
        for block in range(4):
            rows = slice(block * TOK, (block + 1) * TOK)
            start = bound_ref[0:1, rows]
            place = bound_ref[1:2, rows]
            query = q_ref[rows, cols]
            d_out = do_ref[rows, cols]
            lse = lse_ref[head : head + 1, rows]
            delta = jnp.zeros((1, TOK), WIDE)
            probs, d_probs = [], []
            for chunk in range(block + 1):
                keys = chunk_rows(kv_ref, chunk, head * HD, head * HD + HD)
                scores = masked(dot(keys, query, ((1,), (1,))), start, place, chunk, block)
                prob = jnp.exp(scores - lse)
                values = chunk_rows(kv_ref, chunk, WIDTH + head * HD, WIDTH + head * HD + HD)
                d_prob = dot(values, d_out, ((1,), (1,)))
                delta = delta + (prob * d_prob).sum(axis=0, keepdims=True)
                p_ref[chunk * CHUNK : (chunk + 1) * CHUNK, rows] = prob.astype(LOW)
                probs.append(prob)
                d_probs.append(d_prob)
            d_query = jnp.zeros((HD, TOK), WIDE)
            for chunk in range(block + 1):
                d_score = (probs[chunk] * (d_probs[chunk] - delta)).astype(LOW)
                ds_ref[chunk * CHUNK : (chunk + 1) * CHUNK, rows] = d_score
                keys = chunk_rows(kv_ref, chunk, head * HD, head * HD + HD)
                d_query = d_query + dot(keys, d_score, ((0,), (0,)))
            dq_ref[rows, cols] = (jnp.transpose(d_query) * (HD**-0.5)).astype(LOW)
        for chunk in range(4):
            spots = slice(chunk * CHUNK, (chunk + 1) * CHUNK)
            later = slice(chunk * TOK, 4 * TOK)
            d_keys = dot(ds_ref[spots, later], q_ref[later, cols]).astype(LOW)
            d_values = dot(p_ref[spots, later], do_ref[later, cols]).astype(LOW)
            for y in range(4):
                part = slice(y * TOK, (y + 1) * TOK)
                place_rows = slice(chunk * TOK, (chunk + 1) * TOK)
                dkv_ref[y, place_rows, cols] = d_keys[part]
                dkv_ref[y, place_rows, WIDTH + head * HD : WIDTH + head * HD + HD] = d_values[part]


VMEM = pl.BlockSpec(memory_space=pltpu.VMEM)
PARAMS = pltpu.CompilerParams(vmem_limit_bytes=48 * 1024 * 1024)


def attend_forward(query, kv, bounds):
    return pl.pallas_call(
        forward_kernel,
        out_shape=(
            jax.ShapeDtypeStruct((4 * TOK, WIDTH), LOW),
            jax.ShapeDtypeStruct((8, 4 * TOK), WIDE),
        ),
        in_specs=[VMEM] * 3,
        out_specs=(VMEM, VMEM),
        compiler_params=PARAMS,
        cost_estimate=pl.CostEstimate(
            flops=1_000_000_000, bytes_accessed=4_000_000, transcendentals=2_000_000
        ),
    )(query, kv, bounds)


def attend_backward(query, kv, bounds, lse, d_out):
    return pl.pallas_call(
        backward_kernel,
        out_shape=(
            jax.ShapeDtypeStruct((4 * TOK, WIDTH), LOW),
            jax.ShapeDtypeStruct((4, 4 * TOK, 2 * WIDTH), LOW),
        ),
        in_specs=[VMEM] * 5,
        out_specs=(VMEM, VMEM),
        scratch_shapes=[
            pltpu.VMEM((4 * CHUNK, 4 * TOK), LOW),
            pltpu.VMEM((4 * CHUNK, 4 * TOK), LOW),
        ],
        compiler_params=PARAMS,
        cost_estimate=pl.CostEstimate(
            flops=2_500_000_000, bytes_accessed=6_000_000, transcendentals=2_000_000
        ),
    )(query, kv, bounds, lse, d_out)


def norm_parts(values):
    average = jnp.mean(values, axis=-1, keepdims=True)
    centered = values - average
    variance = jnp.mean(centered * centered, axis=-1, keepdims=True)
    inverse = lax.rsqrt(variance + 1e-05)
    return centered * inverse, inverse


def norm_back(hat, inverse, gain, grad):
    scaled = grad * gain
    mean_one = jnp.mean(scaled, axis=-1, keepdims=True)
    mean_two = jnp.mean(scaled * hat, axis=-1, keepdims=True)
    d_values = inverse * (scaled - mean_one - hat * mean_two)
    return d_values, jnp.sum(grad * hat, axis=0), jnp.sum(grad, axis=0)


def swap(value, axis):
    return lax.all_to_all(value, axis, 0, 0, tiled=True)


def sum_swap(value, axis):
    moved = swap(value, axis)
    return jnp.sum(moved.astype(WIDE), axis=0)


def pad_rows(value, count):
    return jnp.pad(value, ((0, count - value.shape[0]), (0, 0)))


def body(
    tokens,
    segments,
    w_qkv,
    w_out,
    w_up,
    w_down,
    b_query,
    b_value,
    b_out,
    b_up,
    b_down,
    ln1_gain,
    ln1_shift,
    ln2_gain,
    ln2_shift,
    cotangent,
):
    ix, ic, iz, iy = (lax.axis_index(name) for name in ("x", "c", "z", "y"))
    first_doc = 3 * (2 * ix + ic)

    counts = jnp.stack(
        [jnp.sum(segments <= first_doc), jnp.sum(segments <= first_doc + 1)]
    ).astype(LOW)
    small = jnp.concatenate(
        [b_query, b_value, b_out, b_down, ln1_gain, ln1_shift, ln2_gain, ln2_shift, b_up]
    )
    small_rows = jnp.stack([small, jnp.pad(counts, (0, small.shape[0] - 2))])
    head_part = w_qkv.reshape(48, 3, 4, WIDTH).transpose(2, 0, 1, 3).reshape(4, 48, 3 * WIDTH)
    early = jnp.concatenate(
        [head_part, jnp.broadcast_to(pad_rows(small_rows, 16)[None], (4, 16, 3 * WIDTH))], axis=1
    )
    early = swap(early, "z")
    early_y = jnp.concatenate(
        [
            early[:, :48].reshape(192, 3 * WIDTH),
            pad_rows(early[:, 48:50].reshape(8, 3 * WIDTH), 16),
        ],
        axis=0,
    )
    early_all = lax.all_gather(early_y, "y")
    qkv_part = early_all[:, :192].reshape(4, 4, 48, 3 * WIDTH).swapaxes(0, 1).reshape(D, 3 * WIDTH)
    small_all = early_all[:, 192:200].reshape(4, 4, 2, 576).swapaxes(0, 1).astype(WIDE)
    vectors = small_all[:, :, 0]
    total_counts = jnp.sum(small_all[:, :, 1, :2], axis=(0, 1)).astype(jnp.int32)
    wide = vectors[:, :, : 8 * 48].reshape(16, 8, 48).swapaxes(0, 1).reshape(8, D)
    bias_out, bias_down, gain_one, shift_one, gain_two, shift_two = (
        wide[index] for index in range(2, 8)
    )
    own = lax.dynamic_index_in_dim(vectors, iz, 0, keepdims=False)
    bias_query = own[:, :48].reshape(WIDTH)
    bias_value = own[:, 48:96].reshape(WIDTH)
    bias_up = own[:, 384:].reshape(D)

    late = jnp.concatenate(
        [
            w_up.reshape(48, 4, D).swapaxes(0, 1),
            jnp.broadcast_to(w_out[None], (4, 48, D)),
        ],
        axis=1,
    )
    late = swap(late, "z")
    late_y = jnp.concatenate(
        [late[:, :48].reshape(192, D), late[:, 48:].reshape(192, D), w_down], axis=0
    )
    late_all = lax.all_gather(late_y, "y")
    up_part = late_all[:, :192].reshape(4, 4, 48, D).swapaxes(0, 1).reshape(D, D)
    out_full = late_all[:, 192:384].reshape(4, 4, 48, D).swapaxes(0, 1).reshape(D, D)
    down_part = late_all[:, 384:].reshape(D, D)

    seg_row = jnp.pad(segments.astype(LOW)[None], ((0, 15), (0, D - TOK)))
    token_all = lax.all_gather(jnp.concatenate([tokens, seg_row], axis=0), "z")
    inputs = token_all[:, :TOK].reshape(4 * TOK, D).astype(WIDE)
    seg_all = token_all[:, TOK, :TOK].astype(jnp.int32)
    cot_all = lax.all_gather(cotangent, "z", tiled=True)
    start = jnp.where(
        seg_all <= first_doc, 0, jnp.where(seg_all <= first_doc + 1, total_counts[0], total_counts[1])
    )
    place = (
        4 * TOK * jnp.arange(4, dtype=jnp.int32)[:, None]
        + TOK * iy
        + jnp.arange(TOK, dtype=jnp.int32)[None, :]
    )
    bounds = jnp.concatenate(
        [start.reshape(1, 4 * TOK), place.reshape(1, 4 * TOK), jnp.zeros((6, 4 * TOK), jnp.int32)]
    )

    hat_one, inverse_one = norm_parts(inputs)
    normed_one = (hat_one * gain_one + shift_one).astype(LOW)
    qkv = dot(normed_one, qkv_part)
    query = ((qkv[:, :WIDTH] + bias_query).astype(LOW) * (HD**-0.5)).astype(LOW)
    kv = jnp.concatenate(
        [qkv[:, WIDTH : 2 * WIDTH], qkv[:, 2 * WIDTH :] + bias_value], axis=1
    ).astype(LOW)
    kv_all = lax.all_gather(kv, "y")
    att_part, lse = attend_forward(query, kv_all, bounds)
    att_all = lax.all_gather(att_part, "z")
    attended = jnp.concatenate([att_all[index] for index in range(4)], axis=1)

    middle = inputs + dot(attended, out_full) + bias_out
    hat_two, inverse_two = norm_parts(middle)
    normed_two = (hat_two * gain_two + shift_two).astype(LOW)
    upward = dot(normed_two, up_part) + bias_up
    activated, pull = jax.vjp(jax.nn.gelu, upward)
    activated = activated.astype(LOW)
    (d_upward,) = pull(dot(cot_all, down_part, ((1,), (1,))))
    d_upward = d_upward.astype(LOW)
    pair = jnp.concatenate(
        [
            dot(activated, down_part).astype(LOW).reshape(4, TOK, D),
            dot(d_upward, up_part, ((1,), (1,))).astype(LOW).reshape(4, TOK, D),
        ],
        axis=2,
    )
    pair = sum_swap(pair, "z")
    own_rows = iz * TOK
    middle_own = lax.dynamic_slice_in_dim(middle, own_rows, TOK, 0)
    out_tokens = (middle_own + pair[:, :D] + bias_down).astype(LOW)
    hat_own = lax.dynamic_slice_in_dim(hat_two, own_rows, TOK, 0)
    inverse_own = lax.dynamic_slice_in_dim(inverse_two, own_rows, TOK, 0)
    d_norm, d_gain_two, d_shift_two = norm_back(hat_own, inverse_own, gain_two, pair[:, D:])
    d_middle = cotangent.astype(WIDE) + d_norm
    d_branch = lax.all_gather(d_middle.astype(LOW), "z", tiled=True)
    out_rows = lax.dynamic_slice_in_dim(out_full, iz * WIDTH, WIDTH, 0)
    d_attended = dot(d_branch, out_rows, ((1,), (1,))).astype(LOW)

    d_up = dot(normed_two, d_upward, ((0,), (0,))).astype(LOW)
    d_down = dot(activated, cot_all, ((0,), (0,))).astype(LOW)
    d_out = dot(att_part, d_branch, ((0,), (0,))).astype(LOW)
    first_grads = jnp.concatenate(
        [
            d_up.reshape(4, 4, 48, D).swapaxes(0, 1).reshape(4, 192, D),
            d_down.reshape(4, 192, D),
            d_out.reshape(4, 48, D),
        ],
        axis=1,
    )
    first_sum = lax.psum_scatter(first_grads, "y", scatter_dimension=0, tiled=False)

    d_query, d_kv = attend_backward(query, kv_all, bounds, lse, d_attended)
    d_kv = sum_swap(d_kv, "y").astype(LOW)
    d_qkv = jnp.concatenate([d_query, d_kv], axis=1)
    d_normed = dot(d_qkv, qkv_part, ((1,), (1,))).astype(LOW).reshape(4, TOK, D)
    d_normed = sum_swap(d_normed, "z")
    hat_own = lax.dynamic_slice_in_dim(hat_one, own_rows, TOK, 0)
    inverse_own = lax.dynamic_slice_in_dim(inverse_one, own_rows, TOK, 0)
    d_norm, d_gain_one, d_shift_one = norm_back(hat_own, inverse_own, gain_one, d_normed)
    d_tokens = (d_middle + d_norm).astype(LOW)
    d_qkv_w = dot(normed_one, d_qkv, ((0,), (0,))).astype(LOW)

    def own_part(vector):
        return lax.dynamic_index_in_dim(vector.reshape(4, 4, 48), iz, 0, keepdims=False)

    d_qkv_sum = jnp.sum(d_qkv.astype(WIDE), axis=0)
    d_bias_out = own_part(jnp.sum(d_branch.astype(WIDE), axis=0))
    d_bias_down = own_part(jnp.sum(cot_all.astype(WIDE), axis=0))
    d_bias_up = jnp.sum(d_upward.astype(WIDE), axis=0).reshape(4, 192)
    norms = jnp.stack([d_gain_one, d_shift_one, d_gain_two, d_shift_two])
    norms = norms.reshape(4, 4, 4, 48).transpose(2, 1, 0, 3).reshape(4, D)
    smalls = jnp.concatenate(
        [
            norms,
            d_qkv_sum[:WIDTH].reshape(4, 48),
            d_qkv_sum[2 * WIDTH :].reshape(4, 48),
            d_bias_out,
            d_bias_down,
            d_bias_up,
        ],
        axis=1,
    ).astype(LOW)
    second_grads = jnp.concatenate(
        [
            d_qkv_w.reshape(4, 4, 48, 3 * WIDTH).swapaxes(0, 1).reshape(4, 192, 3 * WIDTH),
            jnp.pad(smalls.reshape(4, 2, 576), ((0, 0), (0, 14), (0, 0))),
        ],
        axis=1,
    )
    second_sum = sum_swap(second_grads, "y").astype(LOW)

    small_sum = second_sum[192:194].reshape(2 * 576)
    norm_rows = jnp.pad(small_sum[:D].reshape(4, 1, 192), ((0, 0), (0, 15), (0, 3 * WIDTH - 192)))
    moved_qkv = swap(
        jnp.concatenate([second_sum[:192].reshape(4, 48, 3 * WIDTH), norm_rows], axis=1), "z"
    )
    moved_up = swap(first_sum[:192].reshape(4, 48, D), "z")
    norm_sum = jnp.sum(moved_qkv[:, 48, :192].astype(WIDE), axis=0).astype(LOW)
    qkv_rows = (
        moved_qkv[:, :48].reshape(4, 48, 3, WIDTH).transpose(2, 1, 0, 3).reshape(3 * 48, D)
    )
    small_row = jnp.concatenate([norm_sum, small_sum[D:], jnp.zeros((192,), LOW)])
    packed = jnp.concatenate(
        [
            qkv_rows,
            moved_up.reshape(192, D),
            first_sum[192:],
            pad_rows(small_row[None], 64),
        ],
        axis=0,
    )

    halves = packed.reshape(2, 320, D)
    mine = lax.dynamic_index_in_dim(halves, ic, 0, keepdims=False)
    theirs = lax.dynamic_index_in_dim(halves, 1 - ic, 0, keepdims=False)
    got = lax.ppermute(theirs, "c", [(0, 1), (1, 0)])
    half = (mine.astype(WIDE) + got.astype(WIDE)).astype(LOW)
    piece = sum_swap(half.reshape(4, 80, D), "x").astype(LOW)
    half = lax.all_gather(piece, "x", tiled=True)
    whole = lax.all_gather(half, "c", tiled=True).astype(WIDE)

    d_w_qkv = jnp.concatenate([whole[48 * i : 48 * i + 48] for i in range(3)], axis=1)
    d_w_up = jnp.concatenate([whole[144 + 48 * i : 192 + 48 * i] for i in range(4)], axis=1)
    d_w_down = whole[336:528]
    d_w_out = whole[528:576]
    line = whole[576]
    return (
        out_tokens,
        d_tokens,
        d_w_qkv,
        d_w_out,
        d_w_up,
        d_w_down,
        line[192:240],
        line[240:288],
        line[288:336],
        line[384:576],
        line[336:384],
        line[0:48],
        line[48:96],
        line[96:144],
        line[144:192],
    )


def solution(mesh):
    parts = Mesh(mesh.devices.reshape(4, 2, 4, 4), ("x", "c", "z", "y"))
    every = ("x", "c", "z", "y")
    group = ("z", "y")
    row, line = P(group, None), P(group)
    return jax.shard_map(
        body,
        mesh=parts,
        in_specs=(P(every, None), P(every)) + (row,) * 4 + (line,) * 9 + (P(every, None),),
        out_specs=(P(every, None),) * 2 + (row,) * 4 + (line,) * 9,
        check_vma=False,
    )
```

time: 866 us -> 348 us (0.40)
  waiting for transfers between devices: 555 us -> 102 us
  blocking collectives: 165 us -> 104 us
  starting transfers between devices: 0.48 us -> 37.1 us
  matrix products: 46.7 us -> 15.9 us
  Pallas kernels: 0 us -> 14.8 us
  local copies, waits for them, and re-layouts: 43.8 us -> 33.3 us
    reduce_scatter x5 -> x1, waiting for transfers between devices: 308 us -> 0.01 us  [body(): lax.psum_scatter(first_grads, 'y', scatter_dimension=0, tiled=False)]
    all_gather x6 -> x2, waiting for transfers between devices: 185 us -> 29.9 us  [the longest x1 25 us: body(): late_all = lax.all_gather(late_y, 'y')]
    unnamed x2 -> x0, blocking collectives: 121 us -> none
    all_to_all x0 -> x7, waiting for transfers between devices: none -> 70.3 us  [swap(): return lax.all_to_all(value, axis, 0, 0, tiled=True)]
    all_gather x1 -> x7, blocking collectives: 15.6 us -> 80.2 us  [the longest x1 13.9 us: body(): token_all = lax.all_gather(jnp.concatenate([tokens, seg_row], axis=0), 'z')]
    psum x1 -> x0, waiting for transfers between devices: 58.7 us -> none  [body(): lax.psum(shares[0].astype(jnp.bfloat16), 'rep').astype(jnp.float32)]
    dot_general x19 -> x12, matrix products: 46.7 us -> 15.9 us  [dot(): lax.dot_general(left, right, (dims, ((), ())), preferred_element_type=WIDE)]
    all_to_all x0 -> x7, starting transfers between devices: none -> 30 us  [swap(): return lax.all_to_all(value, axis, 0, 0, tiled=True)]
  transfers between devices with their start and end apart: 12 -> 11, of which waited for: 10 -> 9; matrix products, arithmetic and copies ran while one was open for 8% -> 8% of each run, Pallas kernels for 0% -> 4%
where the time goes in v1:
time: 348 us; the launch traced here: 347 us
  blocking collectives  104 us (30%)
  waiting for transfers between devices  102 us (29%)
  starting transfers between devices  37.1 us (11%)
  local copies, waits for them, and re-layouts  33.3 us (10%)
  other arithmetic  23.6 us (7%)
  matrix products  15.9 us (5%)
  between operations  15.9 us (5%)
  Pallas kernels  14.8 us (4%)
    all_to_all x7, waiting for transfers between devices, swap(): return lax.all_to_all(value, axis, 0, 0, tiled=True)  70.3 us
    all_to_all x7, starting transfers between devices, swap(): return lax.all_to_all(value, axis, 0, 0, tiled=True)  30 us
    all_gather x1, waiting for transfers between devices, body(): late_all = lax.all_gather(late_y, 'y')  25 us
    all_to_all x2, blocking collectives, swap(): return lax.all_to_all(value, axis, 0, 0, tiled=True)  23.9 us
    dot_general x12, matrix products, dot(): lax.dot_general(left, right, (dims, ((), ())), preferred_element_type=WIDE)  15.9 us
    all_gather x1, blocking collectives, body(): token_all = lax.all_gather(jnp.concatenate([tokens, seg_row], axis=0), 'z')  13.9 us
    all_gather x1, blocking collectives, body(): early_all = lax.all_gather(early_y, 'y')  12.9 us
    all_gather x1, blocking collectives, body(): cot_all = lax.all_gather(cotangent, 'z', tiled=True)  12.4 us
  transfers between devices with their start and end apart: 11, of which 9 were waited for; matrix products, arithmetic and copies ran while one was open for 8% of the time, Pallas kernels for 4%

profile of v1, /device:TPU:1, one launch (start us, length us, event | category | flops | bytes accessed | tf_op | source)
XLA Modules:
  0.0 346.6 jit_solution(3711626173746615504)
XLA Ops:
  10.0 6.1 %concatenate.73 = bf16[576]{0:T(1024)(128)(2,1)S(1)} concatenate(bf16[48]{0:T(256)(128)(2,1)} %param.22, bf16[48]{0:T(256)(128)(2,1)} %param.23, bf16[48]{0:T(256)(128)(2,1)} %param.24, bf16[48]{0:T(256)(128)(2,1)} %param.26, bf16[48]{0:T(256)(128)(2,1)} %param.27, bf16[48]{0:T(256)(128)(2,1)} %param.28, bf16[48]{0:T(256)(128)(2,1)} %param.29, bf16[48]{0:T(256)(128)(2,1)} %param.30, ...), dimensions={0} | concatenate | bytes 2304 | tf_op jit(solution)/shard_map/concatenate | solution.py:203
  18.6 5.9 %all-to-all-start = ((bf16[4,64,576]{2,1,0:T(8,128)(2,1)}), bf16[4,64,576]{2,1,0:T(8,128)(2,1)S(1)}, u32[]{:S(2)}, u32[]{:S(2)}) async-start(bf16[4,64,576]{2,1,0:T(8,128)(2,1)} %pad_maximum_fusion.8), calls=%async_computation | async-start | bytes 655360 | tf_op jit(solution)/shard_map/all_to_all | solution.py:167
  24.5 13.9 %all-gather = bf16[576,768]{1,0:T(8,128)(2,1)S(1)} all-gather(bf16[144,768]{1,0:T(8,128)(2,1)S(1)} %fusion.43), channel_id=2, replica_groups=mesh['x'=4,'c'=2,'z'=4,'y'=4] {'z'}, dimensions={0}, use_global_device_ids=true | all-gather | bytes 1105920 | tf_op jit(solution)/shard_map/all_gather | solution.py:250
  39.0 12.9 %all-gather.1 = bf16[832,576]{1,0:T(8,128)(2,1)S(1)} all-gather(bf16[208,576]{1,0:T(8,128)(2,1)S(1)} %fusion.41), channel_id=3, replica_groups=mesh['x'=4,'c'=2,'z'=4,'y'=4] {'y'}, dimensions={0}, use_global_device_ids=true | all-gather | bytes 1198080 | tf_op jit(solution)/shard_map/all_gather | solution.py:219
  55.2 10.0 %all_to_all.45 = bf16[4,96,768]{2,1,0:T(8,128)(2,1)S(1)} all-to-all(bf16[4,96,768]{2,1,0:T(8,128)(2,1)S(1)} %pad_maximum_fusion.4), channel_id=1, replica_groups=mesh['x'=4,'c'=2,'z'=4,'y'=4] {'z'}, dimensions={0} | all-to-all | bytes 1179648 | tf_op jit(solution)/shard_map/all_to_all | solution.py:167
  67.4 12.4 %all_gather.49 = bf16[512,768]{1,0:T(8,128)(2,1)} all-gather(bf16[128,768]{1,0:T(8,128)(2,1)S(1)} %copy-done.20), channel_id=1, replica_groups=mesh['x'=4,'c'=2,'z'=4,'y'=4] {'z'}, dimensions={0}, use_global_device_ids=true | all-gather | bytes 983040 | tf_op jit(solution)/shard_map/all_gather | solution.py:253
  82.4 4.8 %all-gather.7.cloned.1.call-done.kv_ref = bf16[4,512,384]{2,1,0:T(8,128)(2,1)} async-done(((bf16[1,512,384]{2,1,0:T(8,128)(2,1)}), bf16[4,512,384]{2,1,0:T(8,128)(2,1)}) %all-gather.7.cloned.1.call-update) | async-done | bytes 1572880 | tf_op jit(solution)/shard_map/all_gather | solution.py:273
  88.6 5.0 %shard_map.271 = (bf16[512,192]{1,0:T(8,128)(2,1)S(1)}, f32[8,512]{1,0:T(8,128)S(1)}) custom-call(bf16[512,192]{1,0:T(8,128)(2,1)S(1)} %fusion.42.q_ref, bf16[4,512,384]{2,1,0:T(8,128)(2,1)S(1)} %copy-done, s32[8,512]{1,0:T(8,128)S(1)} %add_add_fusion.bound_ref), custom_call_target="tpu_custom_call" | custom-call | flops 1000000000 | bytes 4000000 | tf_op jit(solution)/shard_map/pallas_call | solution.py:115
  93.6 12.2 %all-gather.2 = bf16[2048,192]{1,0:T(8,128)(2,1)S(1)} all-gather(bf16[512,192]{1,0:T(8,128)(2,1)S(1)} %get-tuple-element.19), channel_id=4, replica_groups=mesh['x'=4,'c'=2,'z'=4,'y'=4] {'z'}, dimensions={0}, use_global_device_ids=true | all-gather | bytes 983040 | tf_op jit(solution)/shard_map/all_gather | solution.py:275
  106.8 25.0 %all-gather.9.cloned.1.call-done = bf16[2304,768]{1,0:T(8,128)(2,1)} async-done(((bf16[576,768]{1,0:T(8,128)(2,1)}), bf16[2304,768]{1,0:T(8,128)(2,1)}) %all-gather.9.cloned.1.call-update) | async-done | bytes 3538960 | tf_op jit(solution)/shard_map/all_gather | solution.py:244
  154.8 13.4 %all-to-all-done.2 = bf16[4,128,1536]{2,1,0:T(8,128)(2,1)} async-done(((bf16[4,128,1536]{2,1,0:T(8,128)(2,1)}), bf16[4,128,1536]{2,1,0:T(8,128)(2,1)}, u32[]{:S(2)}, u32[]{:S(2)}) %all-to-all-start.2) | async-done | bytes 1572896 | tf_op jit(solution)/shard_map/all_to_all | solution.py:167
  171.2 11.8 %all_gather.50 = bf16[512,768]{1,0:T(8,128)(2,1)S(1)} all-gather(bf16[128,768]{1,0:T(8,128)(2,1)S(1)} %get-tuple-element.38), channel_id=1, replica_groups=mesh['x'=4,'c'=2,'z'=4,'y'=4] {'z'}, dimensions={0}, use_global_device_ids=true | all-gather | bytes 983040 | tf_op jit(solution)/shard_map/all_gather | solution.py:301
  187.6 9.8 %shard_map.272 = (bf16[512,192]{1,0:T(8,128)(2,1)S(1)}, bf16[4,512,384]{2,1,0:T(8,128)(2,1)}) custom-call(bf16[512,192]{1,0:T(8,128)(2,1)S(1)} %fusion.42.q_ref, bf16[4,512,384]{2,1,0:T(8,128)(2,1)S(1)} %copy-done.1, s32[8,512]{1,0:T(8,128)S(1)} %add_add_fusion.bound_ref, f32[8,512]{1,0:T(8,128)S(1)} %get-tuple-element.20.lse_ref, ...), custom_call_target="tpu_custom_call" | custom-call | flops 2500000000 | bytes 6000000 | tf_op jit(solution)/shard_map/pallas_call | solution.py:131
  197.3 4.5 %all-to-all-start.3 = ((bf16[4,512,384]{2,1,0:T(8,128)(2,1)}), bf16[4,512,384]{2,1,0:T(8,128)(2,1)}, u32[]{:S(2)}, u32[]{:S(2)}) async-start(bf16[4,512,384]{2,1,0:T(8,128)(2,1)} %get-tuple-element.22), calls=%async_computation.3 | async-start | bytes 3145728 | tf_op jit(solution)/shard_map/all_to_all | solution.py:167
  203.9 33.2 %all-to-all-done.3 = bf16[4,512,384]{2,1,0:T(8,128)(2,1)} async-done(((bf16[4,512,384]{2,1,0:T(8,128)(2,1)}), bf16[4,512,384]{2,1,0:T(8,128)(2,1)}, u32[]{:S(2)}, u32[]{:S(2)}) %all-to-all-start.3) | async-done | bytes 1572896 | tf_op jit(solution)/shard_map/all_to_all | solution.py:167
  240.6 4.4 %all-to-all-start.4 = ((bf16[4,128,768]{2,1,0:T(8,128)(2,1)}), bf16[4,128,768]{2,1,0:T(8,128)(2,1)S(1)}, u32[]{:S(2)}, u32[]{:S(2)}) async-start(bf16[4,128,768]{2,1,0:T(8,128)(2,1)} %bitcast.179), calls=%async_computation.4 | async-start | bytes 1572864 | tf_op jit(solution)/shard_map/all_to_all | solution.py:167
  249.1 5.6 %all-to-all-done.4 = bf16[4,128,768]{2,1,0:T(8,128)(2,1)S(1)} async-done(((bf16[4,128,768]{2,1,0:T(8,128)(2,1)}), bf16[4,128,768]{2,1,0:T(8,128)(2,1)S(1)}, u32[]{:S(2)}, u32[]{:S(2)}) %all-to-all-start.4) | async-done | bytes 786464 | tf_op jit(solution)/shard_map/all_to_all | solution.py:167
  256.6 13.9 %all_to_all.46 = bf16[4,208,576]{2,1,0:T(8,128)(2,1)S(1)} all-to-all(bf16[4,208,576]{2,1,0:T(8,128)(2,1)S(1)} %fusion.20), channel_id=1, replica_groups=mesh['x'=4,'c'=2,'z'=4,'y'=4] {'y'}, dimensions={0} | all-to-all | bytes 1916928 | tf_op jit(solution)/shard_map/all_to_all | solution.py:167
  275.2 5.7 %all-to-all-done.6 = bf16[4,64,576]{2,1,0:T(8,128)(2,1)S(1)} async-done(((bf16[4,64,576]{2,1,0:T(8,128)(2,1)}), bf16[4,64,576]{2,1,0:T(8,128)(2,1)S(1)}, u32[]{:S(2)}, u32[]{:S(2)}) %all-to-all-start.6) | async-done | bytes 294944 | tf_op jit(solution)/shard_map/all_to_all | solution.py:167
  288.7 4.7 %all-to-all-done.7 = bf16[4,48,768]{2,1,0:T(8,128)(2,1)S(1)} async-done(((bf16[4,48,768]{2,1,0:T(8,128)(2,1)}), bf16[4,48,768]{2,1,0:T(8,128)(2,1)S(1)}, u32[]{:S(2)}, u32[]{:S(2)}) %all-to-all-start.7) | async-done | bytes 294944 | tf_op jit(solution)/shard_map/all_to_all | solution.py:167
  295.2 7.0 %collective-permute-start = (bf16[320,768]{1,0:T(8,128)(2,1)}, bf16[320,768]{1,0:T(8,128)(2,1)}, u32[]{:S(2)}, u32[]{:S(2)}) collective-permute-start(bf16[320,768]{1,0:T(8,128)(2,1)} %dynamic-slice_bitcast_fusion), channel_id=1, source_target_pairs={{0,16},{16,0},{1,17},{17,1},{2,18},{18,2},{3,19},{19,3},{4,20},{20... | collective-permute-start | bytes 1474568 | tf_op jit(solution)/shard_map/ppermute | solution.py:382
  310.7 7.7 %all-to-all-done.8 = bf16[4,80,768]{2,1,0:T(8,128)(2,1)S(1)} async-done(((bf16[4,80,768]{2,1,0:T(8,128)(2,1)}), bf16[4,80,768]{2,1,0:T(8,128)(2,1)S(1)}, u32[]{:S(2)}, u32[]{:S(2)}) %all-to-all-start.8) | async-done | bytes 491552 | tf_op jit(solution)/shard_map/all_to_all | solution.py:167
  318.5 10.7 %all_gather.51 = bf16[320,768]{1,0:T(8,128)(2,1)S(1)} all-gather(bf16[80,768]{1,0:T(8,128)(2,1)S(1)} %reduce_sum.261), channel_id=1, replica_groups=mesh['x'=4,'c'=2,'z'=4,'y'=4] {'x'}, dimensions={0}, use_global_device_ids=true | all-gather | bytes 614400 | tf_op jit(solution)/shard_map/all_gather | solution.py:385
  329.2 6.3 %all_gather.52 = bf16[640,768]{1,0:T(8,128)(2,1)S(1)} all-gather(bf16[320,768]{1,0:T(8,128)(2,1)S(1)} %all_gather.51), channel_id=1, replica_groups=mesh['x'=4,'c'=2,'z'=4,'y'=4] {'c'}, dimensions={0}, use_global_device_ids=true | all-gather | bytes 1474560 | tf_op jit(solution)/shard_map/all_gather | solution.py:386
  (227 shorter events, 83.9 us)
Async XLA Ops:
  16.0 8.4 %copy-start.26 = (bf16[128,768]{1,0:T(8,128)(2,1)S(1)}, bf16[128,768]{1,0:T(8,128)(2,1)}, u32[]{:S(2)}) copy-start(bf16[128,768]{1,0:T(8,128)(2,1)} %param.16) | copy-start | bytes 589828
  18.6 20.3 %all-to-all-start = ((bf16[4,64,576]{2,1,0:T(8,128)(2,1)}), bf16[4,64,576]{2,1,0:T(8,128)(2,1)S(1)}, u32[]{:S(2)}, u32[]{:S(2)}) async-start(bf16[4,64,576]{2,1,0:T(8,128)(2,1)} %pad_maximum_fusion.8), calls=%async_computation | async-start | bytes 655360 | tf_op jit(solution)/shard_map/all_to_all | solution.py:167
  24.4 62.8 %all-gather.7.cloned.1.call-start = ((), (), s32[]{:S(2)}) async-start(), calls=%async_computation.10 | async-start | bytes 1966080 | tf_op jit(solution)/shard_map/all_gather | solution.py:273
  55.0 76.8 %all-gather.9.cloned.1.call-start = ((), (), s32[]{:S(2)}) async-start(), calls=%async_computation.12 | async-start | bytes 4423680 | tf_op jit(solution)/shard_map/all_gather | solution.py:244
  55.1 10.1 %copy-start.21 = (bf16[192,768]{1,0:T(8,128)(2,1)S(1)}, bf16[192,768]{1,0:T(8,128)(2,1)}, u32[]{:S(2)}) copy-start(bf16[192,768]{1,0:T(8,128)(2,1)} %param.21) | copy-start | bytes 884740
  134.2 2.6 copy-start.16
  137.4 1.9 copy-start.9
  143.7 24.4 %all-to-all-start.2 = ((bf16[4,128,1536]{2,1,0:T(8,128)(2,1)}), bf16[4,128,1536]{2,1,0:T(8,128)(2,1)}, u32[]{:S(2)}, u32[]{:S(2)}) async-start(bf16[4,128,1536]{2,1,0:T(8,128)(2,1)} %pad_maximum_fusion.1), calls=%async_computation.2 | async-start | bytes 3145728 | tf_op jit(solution)/shard_map/all_to_all | solution.py:167
  148.1 134.4 %reduce-scatter.2.cloned.1.call-start = ((), (), s32[]{:S(2)}) async-start(), calls=%async_computation.11 | async-start | bytes 3317760 | tf_op jit(solution)/shard_map/reduce_scatter | solution.py:316
  150.7 2.1 copy-start.30
  170.2 13.7 %copy-start.18 = (bf16[768,768]{1,0:T(8,128)(2,1)S(1)}, bf16[768,768]{1,0:T(8,128)(2,1)}, u32[]{:S(2)}) copy-start(bf16[768,768]{1,0:T(8,128)(2,1)} %convolution_convert_fusion) | copy-start | bytes 3538948
  171.2 12.7 %copy-start.4 = (bf16[4,4,48,768]{3,2,0,1:T(8,128)(2,1)S(1)}, bf16[4,4,48,768]{3,2,0,1:T(8,128)(2,1)}, u32[]{:S(2)}) copy-start(bf16[4,4,48,768]{3,2,0,1:T(8,128)(2,1)} %copy.131) | copy-start | bytes 3538948
  197.3 4.5 %copy-start.15 = (bf16[512,768]{1,0:T(8,128)(2,1)S(1)}, bf16[512,768]{1,0:T(8,128)(2,1)}, u32[]{:S(2)}) copy-start(bf16[512,768]{1,0:T(8,128)(2,1)} %all_gather.49) | copy-start | bytes 2359300
  197.3 39.7 %all-to-all-start.3 = ((bf16[4,512,384]{2,1,0:T(8,128)(2,1)}), bf16[4,512,384]{2,1,0:T(8,128)(2,1)}, u32[]{:S(2)}, u32[]{:S(2)}) async-start(bf16[4,512,384]{2,1,0:T(8,128)(2,1)} %get-tuple-element.22), calls=%async_computation.3 | async-start | bytes 3145728 | tf_op jit(solution)/shard_map/all_to_all | solution.py:167
  203.6 35.3 %copy-start.6 = (bf16[4,4,48,576]{3,2,1,0:T(8,128)(2,1)S(1)}, bf16[4,4,48,576]{3,2,1,0:T(8,128)(2,1)}, u32[]{:S(2)}) copy-start(bf16[4,4,48,576]{3,2,1,0:T(8,128)(2,1)} %copy-done.5) | copy-start | bytes 2654212
  240.6 5.0 %copy-start.7 = (f32[512,768]{1,0:T(8,128)S(1)}, f32[512,768]{1,0:T(8,128)}, u32[]{:S(2)}) copy-start(f32[512,768]{1,0:T(8,128)} %fusion.19) | copy-start | bytes 4718596
  240.6 14.2 %all-to-all-start.4 = ((bf16[4,128,768]{2,1,0:T(8,128)(2,1)}), bf16[4,128,768]{2,1,0:T(8,128)(2,1)S(1)}, u32[]{:S(2)}, u32[]{:S(2)}) async-start(bf16[4,128,768]{2,1,0:T(8,128)(2,1)} %bitcast.179), calls=%async_computation.4 | async-start | bytes 1572864 | tf_op jit(solution)/shard_map/all_to_all | solution.py:167
  249.1 6.8 %copy-start.8 = (f32[512,768]{1,0:T(8,128)S(1)}, f32[512,768]{1,0:T(8,128)}, u32[]{:S(2)}) copy-start(f32[512,768]{1,0:T(8,128)} %fusion.19) | copy-start | bytes 4718596
  271.6 9.3 %all-to-all-start.6 = ((bf16[4,64,576]{2,1,0:T(8,128)(2,1)}), bf16[4,64,576]{2,1,0:T(8,128)(2,1)S(1)}, u32[]{:S(2)}, u32[]{:S(2)}) async-start(bf16[4,64,576]{2,1,0:T(8,128)(2,1)} %fusion.38), calls=%async_computation.6 | async-start | bytes 655360 | tf_op jit(solution)/shard_map/all_to_all | solution.py:167
  284.2 9.1 %all-to-all-start.7 = ((bf16[4,48,768]{2,1,0:T(8,128)(2,1)}), bf16[4,48,768]{2,1,0:T(8,128)(2,1)S(1)}, u32[]{:S(2)}, u32[]{:S(2)}) async-start(bf16[4,48,768]{2,1,0:T(8,128)(2,1)} %bitcast.56), calls=%async_computation.8 | async-start | bytes 589824 | tf_op jit(solution)/shard_map/all_to_all | solution.py:167
  294.3 15.6 %copy-start.12 = (f32[128,768]{1,0:T(8,128)S(1)}, f32[128,768]{1,0:T(8,128)}, u32[]{:S(2)}) copy-start(f32[128,768]{1,0:T(8,128)} %copy-done.11) | copy-start | bytes 1179652
  294.3 15.6 %copy-start.17 = (f32[128,768]{1,0:T(8,128)S(1)}, f32[128,768]{1,0:T(8,128)}, u32[]{:S(2)}) copy-start(f32[128,768]{1,0:T(8,128)} %get-tuple-element.39) | copy-start | bytes 1179652
  295.2 8.8 %collective-permute-start = (bf16[320,768]{1,0:T(8,128)(2,1)}, bf16[320,768]{1,0:T(8,128)(2,1)}, u32[]{:S(2)}, u32[]{:S(2)}) collective-permute-start(bf16[320,768]{1,0:T(8,128)(2,1)} %dynamic-slice_bitcast_fusion), channel_id=1, source_target_pairs={{0,16},{16,0},{1,17},{17,1},{2,18},{18,2},{3,19},{19,3},{4,20},{20... | collective-permute-start | bytes 1474568 | tf_op jit(solution)/shard_map/ppermute | solution.py:382
  305.9 12.5 %all-to-all-start.8 = ((bf16[4,80,768]{2,1,0:T(8,128)(2,1)}), bf16[4,80,768]{2,1,0:T(8,128)(2,1)S(1)}, u32[]{:S(2)}, u32[]{:S(2)}) async-start(bf16[4,80,768]{2,1,0:T(8,128)(2,1)} %bitcast.161), calls=%async_computation.9 | async-start | bytes 983040 | tf_op jit(solution)/shard_map/all_to_all | solution.py:167
  (18 other events, 24.8 us)
Sparse Core Ops, SparseCore 0:
  55.1 32.0 all-gather.6
  88.9 42.8 all-gather.8
  185.8 50.0 reduce-scatter.1

commit v2 on v1

v2 whole, which is shorter than its diff:
```python
import jax
import jax.numpy as jnp
from jax import lax
from jax.experimental import pallas as pl
from jax.experimental.pallas import tpu as pltpu
from jax.sharding import Mesh, PartitionSpec as P

HD = 64
TOK = 128
D = 768
HEADS = 3
WIDTH = HEADS * HD
CHUNK = 512
LOW = jnp.bfloat16
WIDE = jnp.float32


def dot(left, right, dims=((1,), (0,))):
    return lax.dot_general(left, right, (dims, ((), ())), preferred_element_type=WIDE)


def masked(scores, start, place, chunk, block):
    if chunk != block and chunk != 0 and block != 3:
        return scores
    spots = lax.broadcasted_iota(jnp.int32, scores.shape, 0) + chunk * CHUNK
    allowed = None
    if chunk == 0 or block == 3:
        allowed = spots >= start
    if chunk == block:
        causal = spots <= place
        allowed = causal if allowed is None else allowed & causal
    return jnp.where(allowed, scores, -1e30)


def chunk_rows(kv_ref, chunk, low, high):
    return jnp.concatenate(
        [kv_ref[y, chunk * TOK : (chunk + 1) * TOK, low:high] for y in range(4)], axis=0
    )


def forward_kernel(q_ref, kv_ref, bound_ref, att_ref, lse_ref):
    for block in range(4):
        rows = slice(block * TOK, (block + 1) * TOK)
        start = bound_ref[0:1, rows]
        place = bound_ref[1:2, rows]
        for head in range(HEADS):
            cols = slice(head * HD, (head + 1) * HD)
            query = q_ref[rows, cols]
            scores = []
            for chunk in range(block + 1):
                keys = chunk_rows(kv_ref, chunk, head * HD, head * HD + HD)
                scores.append(
                    masked(dot(keys, query, ((1,), (1,))), start, place, chunk, block)
                )
            top = scores[0].max(axis=0, keepdims=True)
            for item in scores[1:]:
                top = jnp.maximum(top, item.max(axis=0, keepdims=True))
            total = jnp.zeros((1, TOK), WIDE)
            summed = jnp.zeros((HD, TOK), WIDE)
            for chunk in range(block + 1):
                weights = jnp.exp(scores[chunk] - top)
                total = total + weights.sum(axis=0, keepdims=True)
                values = chunk_rows(kv_ref, chunk, WIDTH + head * HD, WIDTH + head * HD + HD)
                summed = summed + dot(values, weights.astype(LOW), ((0,), (0,)))
            att_ref[rows, cols] = jnp.transpose(summed / total).astype(LOW)
            lse_ref[head : head + 1, rows] = top + jnp.log(total)


def backward_kernel(q_ref, kv_ref, bound_ref, lse_ref, do_ref, dq_ref, dkv_ref, p_ref, ds_ref):
    for head in range(HEADS):
        cols = slice(head * HD, (head + 1) * HD)
        for block in range(4):
            rows = slice(block * TOK, (block + 1) * TOK)
            start = bound_ref[0:1, rows]
            place = bound_ref[1:2, rows]
            query = q_ref[rows, cols]
            d_out = do_ref[rows, cols]
            lse = lse_ref[head : head + 1, rows]
            delta = jnp.zeros((1, TOK), WIDE)
            probs, d_probs = [], []
            for chunk in range(block + 1):
                keys = chunk_rows(kv_ref, chunk, head * HD, head * HD + HD)
                scores = masked(dot(keys, query, ((1,), (1,))), start, place, chunk, block)
                prob = jnp.exp(scores - lse)
                values = chunk_rows(kv_ref, chunk, WIDTH + head * HD, WIDTH + head * HD + HD)
                d_prob = dot(values, d_out, ((1,), (1,)))
                delta = delta + (prob * d_prob).sum(axis=0, keepdims=True)
                p_ref[chunk * CHUNK : (chunk + 1) * CHUNK, rows] = prob.astype(LOW)
                probs.append(prob)
                d_probs.append(d_prob)
            d_query = jnp.zeros((HD, TOK), WIDE)
            for chunk in range(block + 1):
                d_score = (probs[chunk] * (d_probs[chunk] - delta)).astype(LOW)
                ds_ref[chunk * CHUNK : (chunk + 1) * CHUNK, rows] = d_score
                keys = chunk_rows(kv_ref, chunk, head * HD, head * HD + HD)
                d_query = d_query + dot(keys, d_score, ((0,), (0,)))
            dq_ref[rows, cols] = (jnp.transpose(d_query) * (HD**-0.5)).astype(LOW)
        for chunk in range(4):
            spots = slice(chunk * CHUNK, (chunk + 1) * CHUNK)
            later = slice(chunk * TOK, 4 * TOK)
            d_keys = dot(ds_ref[spots, later], q_ref[later, cols]).astype(LOW)
            d_values = dot(p_ref[spots, later], do_ref[later, cols]).astype(LOW)
            for y in range(4):
                part = slice(y * TOK, (y + 1) * TOK)
                place_rows = slice(chunk * TOK, (chunk + 1) * TOK)
                dkv_ref[y, place_rows, cols] = d_keys[part]
                dkv_ref[y, place_rows, WIDTH + head * HD : WIDTH + head * HD + HD] = d_values[part]


def pack_kernel(tokens_ref, qkv_ref, up_ref, short_ref, hidden_ref, seg_ref, out_ref):
    seg = seg_ref[...]
    count_one = jnp.sum((seg <= 0).astype(WIDE), axis=1, keepdims=True)
    count_two = jnp.sum((seg <= 1).astype(WIDE), axis=1, keepdims=True)
    spot = lax.broadcasted_iota(jnp.int32, (1, 192), 1)
    counts = jnp.where(spot == 0, count_one, jnp.where(spot == 1, count_two, 0.0))
    side = jnp.concatenate(
        [
            jnp.concatenate(
                [short_ref[...].astype(WIDE), jnp.zeros((8, 144), WIDE)], axis=1
            ),
            jnp.concatenate(
                [hidden_ref[...].astype(WIDE), jnp.zeros((4, 144), WIDE)], axis=1
            ),
            counts,
            jnp.concatenate([seg.astype(WIDE), jnp.zeros((1, 64), WIDE)], axis=1),
            jnp.zeros((34, 192), WIDE),
        ],
        axis=0,
    ).astype(LOW)
    for part in range(4):
        out_ref[part, 0:TOK, :] = tokens_ref[...]
        for kind in range(3):
            out_ref[part, TOK : TOK + 48, kind * WIDTH : (kind + 1) * WIDTH] = qkv_ref[
                :, kind * D + part * WIDTH : kind * D + (part + 1) * WIDTH
            ]
        out_ref[part, TOK : TOK + 48, 3 * WIDTH : D] = side
        out_ref[part, TOK + 48 : TOK + 96, :] = up_ref[:, part * D : (part + 1) * D]


def unpack_kernel(core_ref, mine_ref, theirs_ref, qkv_ref, out_ref, up_ref, down_ref, *line_refs):
    first = core_ref[0] == 0
    half = D // 2
    short = jnp.zeros((12, 48), WIDE)
    for part in range(4):
        mine = mine_ref[part].astype(WIDE)
        theirs = theirs_ref[part].astype(WIDE)
        sides = (jnp.where(first, mine, theirs), jnp.where(first, theirs, mine))
        rows = slice(24 * (part % 2), 24 * (part % 2) + 24)
        for core in range(2):
            side = sides[core]
            cols = slice(core * half, (core + 1) * half)
            if part < 3:
                down_ref[part * 64 : (part + 1) * 64, cols] = side[96:160]
            else:
                out_ref[:, cols] = side[96:144]
            for quarter in range(4):
                block = side[24 * quarter : 24 * quarter + 24]
                if part < 2:
                    low = quarter * D + core * half
                    up_ref[rows, low : low + half] = block
                    continue
                low = quarter * WIDTH
                if core == 0:
                    qkv_ref[rows, low : low + WIDTH] = block[:, :WIDTH]
                    qkv_ref[rows, D + low : D + low + WIDTH] = block[:, WIDTH:]
                else:
                    qkv_ref[rows, 2 * D + low : 2 * D + low + WIDTH] = block[:, :WIDTH]
                    if part == 2:
                        short = short + block[:12, WIDTH : WIDTH + 48]
    hidden = jnp.concatenate([short[2 + i : 3 + i] for i in range(4)], axis=1)
    lines = [short[i : i + 1] for i in (0, 1, 6)] + [hidden]
    lines += [short[i : i + 1] for i in range(7, 12)]
    for ref, value in zip(line_refs, lines):
        ref[...] = value


VMEM = pl.BlockSpec(memory_space=pltpu.VMEM)
PARAMS = pltpu.CompilerParams(vmem_limit_bytes=48 * 1024 * 1024)


def attend_forward(query, kv, bounds):
    return pl.pallas_call(
        forward_kernel,
        out_shape=(
            jax.ShapeDtypeStruct((4 * TOK, WIDTH), LOW),
            jax.ShapeDtypeStruct((8, 4 * TOK), WIDE),
        ),
        in_specs=[VMEM] * 3,
        out_specs=(VMEM, VMEM),
        compiler_params=PARAMS,
        cost_estimate=pl.CostEstimate(
            flops=1_000_000_000, bytes_accessed=4_000_000, transcendentals=2_000_000
        ),
    )(query, kv, bounds)


def attend_backward(query, kv, bounds, lse, d_out):
    return pl.pallas_call(
        backward_kernel,
        out_shape=(
            jax.ShapeDtypeStruct((4 * TOK, WIDTH), LOW),
            jax.ShapeDtypeStruct((4, 4 * TOK, 2 * WIDTH), LOW),
        ),
        in_specs=[VMEM] * 5,
        out_specs=(VMEM, VMEM),
        scratch_shapes=[
            pltpu.VMEM((4 * CHUNK, 4 * TOK), LOW),
            pltpu.VMEM((4 * CHUNK, 4 * TOK), LOW),
        ],
        compiler_params=PARAMS,
        cost_estimate=pl.CostEstimate(
            flops=2_500_000_000, bytes_accessed=6_000_000, transcendentals=2_000_000
        ),
    )(query, kv, bounds, lse, d_out)


def pack(tokens, w_qkv, w_up, short, hidden, segments):
    return pl.pallas_call(
        pack_kernel,
        out_shape=jax.ShapeDtypeStruct((4, TOK + 96, D), LOW),
        in_specs=[VMEM] * 6,
        out_specs=VMEM,
        compiler_params=PARAMS,
        cost_estimate=pl.CostEstimate(
            flops=1_000_000, bytes_accessed=2_500_000, transcendentals=0
        ),
    )(tokens, w_qkv, w_up, short, hidden, segments)


def unpack(core, mine, theirs):
    return pl.pallas_call(
        unpack_kernel,
        out_shape=tuple(
            jax.ShapeDtypeStruct(shape, WIDE)
            for shape in ((48, 3 * D), (48, D), (48, 4 * D), (192, D))
            + ((1, 48),) * 3
            + ((1, 192),)
            + ((1, 48),) * 5
        ),
        in_specs=[pl.BlockSpec(memory_space=pltpu.SMEM), VMEM, VMEM],
        out_specs=(VMEM,) * 13,
        compiler_params=PARAMS,
        cost_estimate=pl.CostEstimate(
            flops=1_000_000, bytes_accessed=3_500_000, transcendentals=0
        ),
    )(core, mine, theirs)


def norm_parts(values):
    average = jnp.mean(values, axis=-1, keepdims=True)
    centered = values - average
    variance = jnp.mean(centered * centered, axis=-1, keepdims=True)
    inverse = lax.rsqrt(variance + 1e-05)
    return centered * inverse, inverse


def norm_back(hat, inverse, gain, grad):
    scaled = grad * gain
    mean_one = jnp.mean(scaled, axis=-1, keepdims=True)
    mean_two = jnp.mean(scaled * hat, axis=-1, keepdims=True)
    return inverse * (scaled - mean_one - hat * mean_two)


def swap(value, axis):
    return lax.all_to_all(value, axis, 0, 0, tiled=True)


def share(value, axis):
    return swap(jnp.broadcast_to(value[None], (4,) + value.shape), axis)


def total(value):
    return jnp.sum(value.astype(WIDE), axis=0)


def other_core(value):
    return lax.ppermute(value, "c", [(0, 1), (1, 0)])


def body(
    tokens,
    segments,
    w_qkv,
    w_out,
    w_up,
    w_down,
    b_query,
    b_value,
    b_out,
    b_up,
    b_down,
    ln1_gain,
    ln1_shift,
    ln2_gain,
    ln2_shift,
    cotangent,
):
    ix, ic, iz, iy = (lax.axis_index(name) for name in ("x", "c", "z", "y"))
    first_doc = 3 * (2 * ix + ic)
    half = D // 2

    def lanes(value, core):
        return lax.dynamic_slice_in_dim(value, core * half, half, value.ndim - 1)

    short = jnp.stack(
        [b_query, b_value, b_out, b_down, ln1_gain, ln1_shift, ln2_gain, ln2_shift]
    )
    early = pack(
        tokens, w_qkv, w_up, short, b_up.reshape(4, 48), (segments - first_doc)[None]
    )
    early = swap(early, "z")
    token_all = early[:, :TOK].reshape(4 * TOK, D)
    seg_all = early[:, TOK + 13, 576:704].astype(jnp.int32)
    early_all = share(early[:, TOK : TOK + 48, :640], "y").swapaxes(0, 1)
    qkv_part = early_all[:, :, :, :576].reshape(D, 3 * WIDTH)
    small_all = early_all[:, :, :16, 576:624].astype(WIDE)
    total_counts = jnp.sum(small_all[:, :, 12, :2], axis=(0, 1)).astype(jnp.int32)
    wide = small_all.reshape(16, 16, 48)[:, :8].swapaxes(0, 1).reshape(8, D)
    bias_out, bias_down, gain_one, shift_one, gain_two, shift_two = (
        wide[index] for index in range(2, 8)
    )
    own = lax.dynamic_index_in_dim(small_all, iz, 0, keepdims=False)
    bias_query = own[:, 0].reshape(WIDTH)
    bias_value = own[:, 1].reshape(WIDTH)
    bias_up = own[:, 8:12].reshape(D)

    plain = lax.all_gather(jnp.concatenate([w_down, w_out], axis=0), "y")
    down_part = plain[:, :192].reshape(D, D)
    gathered = lax.all_gather(
        jnp.concatenate([cotangent, plain[:, 192:].reshape(192, D)], axis=0), "z"
    )
    cot_all = gathered[:, :TOK].reshape(4 * TOK, D)
    out_full = gathered[:, TOK:].reshape(D, D)
    up_part = lax.all_gather(early[:, TOK + 48 :].reshape(192, D), "y")
    up_part = up_part.reshape(4, 4, 48, D).swapaxes(0, 1).reshape(D, D)

    inputs = token_all.astype(WIDE)
    start = jnp.where(
        seg_all <= 0, 0, jnp.where(seg_all <= 1, total_counts[0], total_counts[1])
    )
    place = (
        4 * TOK * jnp.arange(4, dtype=jnp.int32)[:, None]
        + TOK * iy
        + jnp.arange(TOK, dtype=jnp.int32)[None, :]
    )
    bounds = jnp.concatenate(
        [start.reshape(1, 4 * TOK), place.reshape(1, 4 * TOK), jnp.zeros((6, 4 * TOK), jnp.int32)]
    )

    hat_one, inverse_one = norm_parts(inputs)
    normed_one = (hat_one * gain_one + shift_one).astype(LOW)
    qkv = dot(normed_one, qkv_part)
    query = ((qkv[:, :WIDTH] + bias_query).astype(LOW) * (HD**-0.5)).astype(LOW)
    kv = jnp.concatenate(
        [qkv[:, WIDTH : 2 * WIDTH], qkv[:, 2 * WIDTH :] + bias_value], axis=1
    ).astype(LOW)
    kv_all = share(kv, "y")
    att_part, lse = attend_forward(query, kv_all, bounds)
    att_all = share(att_part, "z")
    attended = jnp.concatenate([att_all[index] for index in range(4)], axis=1)

    middle = inputs + dot(attended, out_full) + bias_out
    hat_two, inverse_two = norm_parts(middle)
    normed_two = (hat_two * gain_two + shift_two).astype(LOW)
    upward = dot(normed_two, up_part) + bias_up
    activated, pull = jax.vjp(jax.nn.gelu, upward)
    activated = activated.astype(LOW)
    (d_upward,) = pull(dot(cot_all, down_part, ((1,), (1,))))
    d_upward = d_upward.astype(LOW)
    d_normed = dot(d_upward, up_part, ((1,), (1,)))
    d_gain_two = jnp.sum(d_normed * hat_two, axis=0)
    d_shift_two = jnp.sum(d_normed, axis=0)
    d_normed = total(swap(d_normed.astype(LOW).reshape(4, TOK, D), "z"))
    own_rows = iz * TOK

    def mine(value):
        return lax.dynamic_slice_in_dim(value, own_rows, TOK, 0)

    out_part = dot(activated, down_part).astype(LOW).reshape(4, TOK, D)
    d_middle = cotangent.astype(WIDE) + norm_back(
        mine(hat_two), mine(inverse_two), gain_two, d_normed
    )
    d_branch = d_middle.astype(LOW)
    branch_all = share(d_branch, "z").reshape(4 * TOK, D)
    out_rows = lax.dynamic_slice_in_dim(out_full, iz * WIDTH, WIDTH, 0)
    d_attended = dot(branch_all, out_rows, ((1,), (1,))).astype(LOW)

    def pair_sum(left, right):
        sent = dot(left, lanes(right, 1 - ic), ((0,), (0,))).astype(LOW)
        kept = dot(left, lanes(right, ic), ((0,), (0,)))
        return (kept + other_core(sent).astype(WIDE)).astype(LOW)

    d_up = pair_sum(normed_two, d_upward).reshape(4, 4, 48, half).swapaxes(0, 1)
    first = jnp.concatenate(
        [
            d_up.reshape(4, 192, half),
            pair_sum(activated, cot_all).reshape(4, 192, half),
            pair_sum(att_part, branch_all).reshape(4, 48, half),
        ],
        axis=1,
    )
    first = lax.psum_scatter(first, "y", scatter_dimension=0)
    rows = jnp.pad(first[192:], ((0, 16), (0, 0))).reshape(4, 64, half)
    rows = lax.psum_scatter(rows, "x", scatter_dimension=0)

    d_query, d_kv = attend_backward(query, kv_all, bounds, lse, d_attended)
    d_kv = total(swap(d_kv, "y")).astype(LOW)
    d_qkv = jnp.concatenate([d_query, d_kv], axis=1)
    d_normed = dot(d_qkv, qkv_part, ((1,), (1,)))
    d_gain_one = jnp.sum(d_normed * hat_one, axis=0)
    d_shift_one = jnp.sum(d_normed, axis=0)
    last = jnp.concatenate([d_normed.astype(LOW).reshape(4, TOK, D), out_part], axis=2)
    last = lax.psum_scatter(last, "z", scatter_dimension=0).astype(WIDE)
    d_normed = last[:, :D]
    out_tokens = (mine(middle) + last[:, D:] + bias_down).astype(LOW)
    d_tokens = (
        d_middle + norm_back(mine(hat_one), mine(inverse_one), gain_one, d_normed)
    ).astype(LOW)
    d_qkv_w = dot(normed_one, d_qkv, ((0,), (0,))).astype(LOW)

    d_qkv_sum = jnp.sum(d_qkv.astype(WIDE), axis=0)
    here = (jnp.arange(4) == iz).astype(WIDE)[:, None, None, None]
    of_z = jnp.concatenate(
        [
            d_qkv_sum[:WIDTH].reshape(4, 1, 48),
            d_qkv_sum[2 * WIDTH :].reshape(4, 1, 48),
            jnp.sum(d_upward.astype(WIDE), axis=0).reshape(4, 4, 48),
        ],
        axis=1,
    )
    of_all = jnp.stack(
        [
            jnp.sum(d_branch.astype(WIDE), axis=0),
            jnp.sum(cotangent.astype(WIDE), axis=0),
            d_gain_one,
            d_shift_one,
            d_gain_two,
            d_shift_two,
        ]
    )
    smalls = jnp.concatenate(
        [
            (of_z[None] * here).reshape(16, 6, 48),
            of_all.reshape(6, 16, 48).swapaxes(0, 1),
        ],
        axis=1,
    )
    smalls = jnp.pad(smalls.astype(LOW), ((0, 0), (0, 36), (0, 144)))
    second = jnp.concatenate([d_qkv_w.reshape(16, 48, 576), smalls], axis=2)
    got = other_core(lanes(second, 1 - ic))
    second = (lanes(second, ic).astype(WIDE) + got.astype(WIDE)).astype(LOW)
    second = second.reshape(4, 4, 48, half).swapaxes(0, 1).reshape(4, 192, half)
    second = total(swap(second, "y")).astype(LOW)

    joint = jnp.concatenate(
        [first[:192].reshape(4, 48, half), second.reshape(4, 48, half)], axis=1
    )
    joint = joint.reshape(4, 4, 24, half).swapaxes(0, 1).reshape(16, 24, half)
    joint = total(swap(joint, ("x", "z")).reshape(4, 4, 24, half)).astype(LOW)
    whole = share(jnp.concatenate([joint.reshape(96, half), rows], axis=0), "x")
    theirs = other_core(whole)
    grads = unpack(ic.astype(jnp.int32)[None], whole, theirs)
    return (out_tokens, d_tokens) + grads[:4] + tuple(item[0] for item in grads[4:])


def solution(mesh):
    parts = Mesh(mesh.devices.reshape(4, 2, 4, 4), ("x", "c", "z", "y"))
    every = ("x", "c", "z", "y")
    group = ("z", "y")
    row, line = P(group, None), P(group)
    return jax.shard_map(
        body,
        mesh=parts,
        in_specs=(P(every, None), P(every)) + (row,) * 4 + (line,) * 9 + (P(every, None),),
        out_specs=(P(every, None),) * 2 + (row,) * 4 + (line,) * 9,
        check_vma=False,
    )
```

time: 348 us -> 282 us (0.81)
  blocking collectives: 104 us -> 35.4 us
  waiting for transfers between devices: 102 us -> 79.9 us
  matrix products: 15.9 us -> 26.9 us
  starting transfers between devices: 37.1 us -> 43.2 us
    all_gather x7 -> x0, blocking collectives: 80.2 us -> none  [the longest x1 13.9 us: body(): token_all = lax.all_gather(jnp.concatenate([tokens, seg_row], axis=0), 'z')]
    all_gather x2 -> x3, waiting for transfers between devices: 29.9 us -> 0.02 us  [the longest x1 0.02 us: body(): plain = lax.all_gather(jnp.concatenate([w_down, w_out], axis=0), 'y')]
    all_to_all x2 -> x3, blocking collectives: 23.9 us -> 35.4 us  [swap(): return lax.all_to_all(value, axis, 0, 0, tiled=True)]
    dot_general x12 -> x15, matrix products: 15.9 us -> 26.9 us  [dot(): lax.dot_general(left, right, (dims, ((), ())), preferred_element_type=WIDE)]
    all_to_all x7, waiting for transfers between devices: 70.3 us -> 77.2 us  [swap(): return lax.all_to_all(value, axis, 0, 0, tiled=True)]
    concatenate x2 -> x0, local copies, waits for them, and re-layouts: 6.19 us -> none  [the longest x1 6.08 us: body(): jnp.concatenate([b_query, b_value, b_out, b_down, ln1_gain, ln1_shift, ln...]
    broadcast_in_dim x4 -> x5, local copies, waits for them, and re-layouts: 0.04 us -> 5.29 us  [share(): return swap(jnp.broadcast_to(value[None], (4,) + value.shape), axis)]
    ppermute x1 -> x5, starting transfers between devices: 7 us -> 11.9 us  [other_core(): return lax.ppermute(value, 'c', [(0, 1), (1, 0)])]
  transfers between devices with their start and end apart: 11 -> 18, of which waited for: 9 -> 9; matrix products, arithmetic and copies ran while one was open for 8% -> 23% of each run, Pallas kernels for 4% -> 6%
where the time goes in v2:
time: 282 us; the launch traced here: 280 us
  waiting for transfers between devices  79.9 us (28%)
  starting transfers between devices  43.2 us (15%)
  local copies, waits for them, and re-layouts  36.5 us (13%)
  blocking collectives  35.4 us (13%)
  matrix products  26.9 us (10%)
  other arithmetic  25.6 us (9%)
  Pallas kernels  17.4 us (6%)
  between operations  14.9 us (5%)
    all_to_all x7, waiting for transfers between devices, swap(): return lax.all_to_all(value, axis, 0, 0, tiled=True)  77.2 us
    all_to_all x3, blocking collectives, swap(): return lax.all_to_all(value, axis, 0, 0, tiled=True)  35.4 us
    all_to_all x7, starting transfers between devices, swap(): return lax.all_to_all(value, axis, 0, 0, tiled=True)  30.8 us
    dot_general x15, matrix products, dot(): lax.dot_general(left, right, (dims, ((), ())), preferred_element_type=WIDE)  26.9 us
    ppermute x5, starting transfers between devices, other_core(): return lax.ppermute(value, 'c', [(0, 1), (1, 0)])  11.9 us
    pallas_call x1, Pallas kernels, attend_backward(): pl.pallas_call(backward_kernel, out_shape=(jax.ShapeDtypeStruct((4 * TOK,...  9.82 us
    unnamed x61, local copies, waits for them, and re-layouts  6.41 us
  transfers between devices with their start and end apart: 18, of which 9 were waited for; matrix products, arithmetic and copies ran while one was open for 23% of the time, Pallas kernels for 6%

profile of v2, /device:TPU:1, one launch (start us, length us, event | category | flops | bytes accessed | tf_op | source)
XLA Modules:
  0.0 279.7 jit_solution(6175789338814275371)
XLA Ops:
  15.3 5.9 %all-to-all-start = ((bf16[4,224,768]{2,1,0:T(8,128)(2,1)}), bf16[4,224,768]{2,1,0:T(8,128)(2,1)S(1)}, u32[]{:S(2)}, u32[]{:S(2)}) async-start(bf16[4,224,768]{2,1,0:T(8,128)(2,1)} %shard_map.271), calls=%async_computation | async-start | bytes 2752512 | tf_op jit(solution)/shard_map/all_to_all | solution.py:265
  21.2 17.7 %all-to-all-done = bf16[4,224,768]{2,1,0:T(8,128)(2,1)S(1)} async-done(((bf16[4,224,768]{2,1,0:T(8,128)(2,1)}), bf16[4,224,768]{2,1,0:T(8,128)(2,1)S(1)}, u32[]{:S(2)}, u32[]{:S(2)}) %all-to-all-start) | async-done | bytes 1376288 | tf_op jit(solution)/shard_map/all_to_all | solution.py:265
  40.0 4.2 %all-to-all-start.1 = ((bf16[4,4,48,640]{3,2,1,0:T(8,128)(2,1)}), bf16[4,4,48,640]{3,2,1,0:T(8,128)(2,1)S(1)}, u32[]{:S(2)}, u32[]{:S(2)}) async-start(bf16[4,4,48,640]{3,2,1,0:T(8,128)(2,1)} %broadcast_in_dim.27), calls=%async_computation.1 | async-start | bytes 1966080 | tf_op jit(solution)/shard_map/all_to_all | solution.py:265
  46.8 9.4 %all-to-all-done.1 = bf16[4,4,48,640]{3,2,1,0:T(8,128)(2,1)S(1)} async-done(((bf16[4,4,48,640]{3,2,1,0:T(8,128)(2,1)}), bf16[4,4,48,640]{3,2,1,0:T(8,128)(2,1)S(1)}, u32[]{:S(2)}, u32[]{:S(2)}) %all-to-all-start.1) | async-done | bytes 983072 | tf_op jit(solution)/shard_map/all_to_all | solution.py:265
  63.0 3.6 %all-to-all-start.2 = ((bf16[4,512,384]{2,1,0:T(8,128)(2,1)}), bf16[4,512,384]{2,1,0:T(8,128)(2,1)S(1)}, u32[]{:S(2)}, u32[]{:S(2)}) async-start(bf16[4,512,384]{2,1,0:T(8,128)(2,1)} %broadcast_in_dim.28), calls=%async_computation.2 | async-start | bytes 3145728 | tf_op jit(solution)/shard_map/all_to_all | solution.py:265
  71.8 13.7 %all-to-all-done.2.kv_ref = bf16[4,512,384]{2,1,0:T(8,128)(2,1)S(1)} async-done(((bf16[4,512,384]{2,1,0:T(8,128)(2,1)}), bf16[4,512,384]{2,1,0:T(8,128)(2,1)S(1)}, u32[]{:S(2)}, u32[]{:S(2)}) %all-to-all-start.2) | async-done | bytes 1572896 | tf_op jit(solution)/shard_map/all_to_all | solution.py:265
  85.5 5.0 %shard_map.272 = (bf16[512,192]{1,0:T(8,128)(2,1)S(1)}, f32[8,512]{1,0:T(8,128)S(1)}) custom-call(bf16[512,192]{1,0:T(8,128)(2,1)S(1)} %fusion.50.q_ref, bf16[4,512,384]{2,1,0:T(8,128)(2,1)S(1)} %all-to-all-done.2.kv_ref, s32[8,512]{1,0:T(8,128)S(1)} %add_add_fusion.bound_ref), custom_call_target="tpu_custom_call" | custom-call | flops 1000000000 | bytes 4000000 | tf_op jit(solution)/shard_map/pallas_call | solution.py:182
  93.2 5.8 %all-to-all-start.3 = ((bf16[4,512,192]{1,2,0:T(8,128)(2,1)}), bf16[4,512,192]{1,2,0:T(8,128)(2,1)}, u32[]{:S(2)}, u32[]{:S(2)}) async-start(bf16[4,512,192]{1,2,0:T(8,128)(2,1)} %broadcast_in_dim.32), calls=%async_computation.3 | async-start | bytes 1572864 | tf_op jit(solution)/shard_map/all_to_all | solution.py:265
  106.1 10.2 %all-to-all-done.3 = bf16[4,512,192]{1,2,0:T(8,128)(2,1)} async-done(((bf16[4,512,192]{1,2,0:T(8,128)(2,1)}), bf16[4,512,192]{1,2,0:T(8,128)(2,1)}, u32[]{:S(2)}, u32[]{:S(2)}) %all-to-all-start.3) | async-done | bytes 786464 | tf_op jit(solution)/shard_map/all_to_all | solution.py:265
  126.3 2.8 %convert_reduce_fusion.1 = (f32[768]{0:T(1024)S(1)}, bf16[512,768]{1,0:T(8,128)(2,1)S(1)}, f32[512,768]{1,0:T(8,128)}) fusion(f32[512,768]{1,0:T(8,128)S(1)} %fusion.77, f32[768]{0:T(1024)S(1)} %add.234, bf16[512,768]{1,0:T(8,128)(2,1)S(1)} %get-tuple-element.70, bf16[768,768]{1,0:T(8,128)(2,1)S(1)} %bitcast.129), kind=kOutput, calls=%fused_computation.24 | convolution fusion | flops 613022976 | bytes 5904384 | tf_op jit(solution)/shard_map/dot_general | solution.py:19
  130.9 3.5 %all-to-all-start.4 = ((bf16[4,128,768]{2,1,0:T(8,128)(2,1)}), bf16[4,128,768]{2,1,0:T(8,128)(2,1)S(1)}, u32[]{:S(2)}, u32[]{:S(2)}) async-start(bf16[4,128,768]{2,1,0:T(8,128)(2,1)} %bitcast.34), calls=%async_computation.4 | async-start | bytes 1572864 | tf_op jit(solution)/shard_map/all_to_all | solution.py:265
  134.4 3.0 %convolution_convert_fusion.2 = bf16[768,384]{1,0:T(8,128)(2,1)} fusion(bf16[512,768]{1,0:T(8,128)(2,1)} %bitcast.153, s32[]{:T(128)S(6)} %select_n.59, f32[512,768]{1,0:T(8,128)} %get-tuple-element.94), kind=kOutput, calls=%fused_computation.37 | convolution fusion | flops 305823744 | bytes 2555908 | tf_op jit(solution)/shard_map/dot_general | solution.py:19
  138.7 6.8 %all-to-all-done.4 = bf16[4,128,768]{2,1,0:T(8,128)(2,1)S(1)} async-done(((bf16[4,128,768]{2,1,0:T(8,128)(2,1)}), bf16[4,128,768]{2,1,0:T(8,128)(2,1)S(1)}, u32[]{:S(2)}, u32[]{:S(2)}) %all-to-all-start.4) | async-done | bytes 786464 | tf_op jit(solution)/shard_map/all_to_all | solution.py:265
  150.2 3.5 %all-to-all-start.5 = ((bf16[4,128,768]{2,1,0:T(8,128)(2,1)}), bf16[4,128,768]{2,1,0:T(8,128)(2,1)S(1)}, u32[]{:S(2)}, u32[]{:S(2)}) async-start(bf16[4,128,768]{2,1,0:T(8,128)(2,1)} %broadcast_in_dim.33), calls=%async_computation.5 | async-start | bytes 1572864 | tf_op jit(solution)/shard_map/all_to_all | solution.py:265
  163.9 3.6 %collective-permute-start.2 = (bf16[192,384]{1,0:T(8,128)(2,1)S(1)}, bf16[192,384]{1,0:T(8,128)(2,1)S(1)}, u32[]{:S(2)}, u32[]{:S(2)}) collective-permute-start(bf16[192,384]{1,0:T(8,128)(2,1)S(1)} %convolution_convert_fusion.5), channel_id=1, source_target_pairs={{0,16},{16,0},{1,17},{17,1},{2,18},{18,2},{3,19},{19,3},{4,20},{20... | collective-permute-start | bytes 442376 | tf_op jit(solution)/shard_map/ppermute | solution.py:277
  172.8 9.8 %shard_map.273 = (bf16[512,192]{1,0:T(8,128)(2,1)S(1)}, bf16[4,512,384]{2,1,0:T(8,128)(2,1)}) custom-call(bf16[512,192]{1,0:T(8,128)(2,1)S(1)} %fusion.50.q_ref, bf16[4,512,384]{2,1,0:T(8,128)(2,1)S(1)} %all-to-all-done.2.kv_ref, s32[8,512]{1,0:T(8,128)S(1)} %add_add_fusion.bound_ref, f32[8,512]{1,0:T(8,128)S(1)} %get-tuple-element.33.lse_ref, ...), custom_call_target="tpu_custom_call" | custom-call | flops 2500000000 | bytes 6000000 | tf_op jit(solution)/shard_map/pallas_call | solution.py:198
  182.6 4.5 %all-to-all-start.6 = ((bf16[4,512,384]{2,1,0:T(8,128)(2,1)}), bf16[4,512,384]{2,1,0:T(8,128)(2,1)}, u32[]{:S(2)}, u32[]{:S(2)}) async-start(bf16[4,512,384]{2,1,0:T(8,128)(2,1)} %get-tuple-element.35), calls=%async_computation.6 | async-start | bytes 3145728 | tf_op jit(solution)/shard_map/all_to_all | solution.py:265
  188.9 3.4 %convolution_convert_fusion.1 = bf16[512,768]{1,0:T(8,128)(2,1)} fusion(bf16[768,768]{1,0:T(8,128)(2,1)S(1)} %bitcast.145, f32[512,768]{1,0:T(8,128)} %get-tuple-element.94), kind=kOutput, calls=%fused_computation.35 | convolution fusion | flops 607911936 | bytes 3538944 | tf_op jit(solution)/shard_map/dot_general | solution.py:19
  193.3 16.9 %all-to-all-done.6 = bf16[4,512,384]{2,1,0:T(8,128)(2,1)} async-done(((bf16[4,512,384]{2,1,0:T(8,128)(2,1)}), bf16[4,512,384]{2,1,0:T(8,128)(2,1)}, u32[]{:S(2)}, u32[]{:S(2)}) %all-to-all-start.6) | async-done | bytes 1572896 | tf_op jit(solution)/shard_map/all_to_all | solution.py:265
  216.3 2.7 pad_maximum_fusion
  226.2 12.1 %all_to_all.50 = bf16[4,192,384]{2,1,0:T(8,128)(2,1)S(1)} all-to-all(bf16[4,192,384]{2,1,0:T(8,128)(2,1)S(1)} %bitcast.135), channel_id=1, replica_groups=mesh['x'=4,'c'=2,'z'=4,'y'=4] {'y'}, dimensions={0} | all-to-all | bytes 1179648 | tf_op jit(solution)/shard_map/all_to_all | solution.py:265
  238.6 14.0 %all_to_all.51 = bf16[16,24,384]{2,1,0:T(8,128)(2,1)S(1)} all-to-all(bf16[16,24,384]{2,1,0:T(8,128)(2,1)S(1)} %bitcast.150), channel_id=1, replica_groups=mesh['x'=4,'c'=2,'z'=4,'y'=4] {'x','z'}, dimensions={0} | all-to-all | bytes 589824 | tf_op jit(solution)/shard_map/all_to_all | solution.py:265
  253.5 9.3 %all_to_all.52.mine_ref = bf16[4,160,384]{2,1,0:T(8,128)(2,1)S(1)} all-to-all(bf16[4,160,384]{2,1,0:T(8,128)(2,1)S(1)} %broadcast_in_dim.35), channel_id=1, replica_groups=mesh['x'=4,'c'=2,'z'=4,'y'=4] {'x'}, dimensions={0} | all-to-all | bytes 983040 | tf_op jit(solution)/shard_map/all_to_all | solution.py:265
  262.8 4.1 %collective-permute-start.4 = (bf16[4,160,384]{2,1,0:T(8,128)(2,1)S(1)}, bf16[4,160,384]{2,1,0:T(8,128)(2,1)S(1)}, u32[]{:S(2)}, u32[]{:S(2)}) collective-permute-start(bf16[4,160,384]{2,1,0:T(8,128)(2,1)S(1)} %all_to_all.52.mine_ref), channel_id=1, source_target_pairs={{0,16},{16,0},{1,17},{17,1},{2,18},{18,2},{3,19},{19,3},{4,20},{20... | collective-permute-start | bytes 1474568 | tf_op jit(solution)/shard_map/ppermute | solution.py:277
  (210 shorter events, 89.4 us)
Async XLA Ops:
  7.2 50.6 %all-gather.8.cloned.1.call-start = ((), (), s32[]{:S(2)}) async-start(), calls=%async_computation.17 | async-start | bytes 1843200 | tf_op jit(solution)/shard_map/all_gather | solution.py:327
  15.3 23.6 %all-to-all-start = ((bf16[4,224,768]{2,1,0:T(8,128)(2,1)}), bf16[4,224,768]{2,1,0:T(8,128)(2,1)S(1)}, u32[]{:S(2)}, u32[]{:S(2)}) async-start(bf16[4,224,768]{2,1,0:T(8,128)(2,1)} %shard_map.271), calls=%async_computation | async-start | bytes 2752512 | tf_op jit(solution)/shard_map/all_to_all | solution.py:265
  38.9 60.1 %copy-start.3 = (bf16[4,224,768]{2,1,0:T(8,128)(2,1)}, bf16[4,224,768]{2,1,0:T(8,128)(2,1)S(1)}, u32[]{:S(2)}) copy-start(bf16[4,224,768]{2,1,0:T(8,128)(2,1)S(1)} %all-to-all-done) | copy-start | bytes 4128772
  40.0 16.2 %all-to-all-start.1 = ((bf16[4,4,48,640]{3,2,1,0:T(8,128)(2,1)}), bf16[4,4,48,640]{3,2,1,0:T(8,128)(2,1)S(1)}, u32[]{:S(2)}, u32[]{:S(2)}) async-start(bf16[4,4,48,640]{3,2,1,0:T(8,128)(2,1)} %broadcast_in_dim.27), calls=%async_computation.1 | async-start | bytes 1966080 | tf_op jit(solution)/shard_map/all_to_all | solution.py:265
  44.2 59.6 %all-gather.6.cloned.1.call-start = ((), (), s32[]{:S(2)}) async-start(), calls=%async_computation.13 | async-start | bytes 1474560 | tf_op jit(solution)/shard_map/all_gather | solution.py:334
  45.0 73.4 %all-gather.10.cloned.1.call-start = ((), (), s32[]{:S(2)}) async-start(), calls=%async_computation.18 | async-start | bytes 2457600 | tf_op jit(solution)/shard_map/all_gather | solution.py:329
  63.0 22.5 %all-to-all-start.2 = ((bf16[4,512,384]{2,1,0:T(8,128)(2,1)}), bf16[4,512,384]{2,1,0:T(8,128)(2,1)S(1)}, u32[]{:S(2)}, u32[]{:S(2)}) async-start(bf16[4,512,384]{2,1,0:T(8,128)(2,1)} %broadcast_in_dim.28), calls=%async_computation.2 | async-start | bytes 3145728 | tf_op jit(solution)/shard_map/all_to_all | solution.py:265
  93.2 23.2 %all-to-all-start.3 = ((bf16[4,512,192]{1,2,0:T(8,128)(2,1)}), bf16[4,512,192]{1,2,0:T(8,128)(2,1)}, u32[]{:S(2)}, u32[]{:S(2)}) async-start(bf16[4,512,192]{1,2,0:T(8,128)(2,1)} %broadcast_in_dim.32), calls=%async_computation.3 | async-start | bytes 1572864 | tf_op jit(solution)/shard_map/all_to_all | solution.py:265
  130.9 14.6 %all-to-all-start.4 = ((bf16[4,128,768]{2,1,0:T(8,128)(2,1)}), bf16[4,128,768]{2,1,0:T(8,128)(2,1)S(1)}, u32[]{:S(2)}, u32[]{:S(2)}) async-start(bf16[4,128,768]{2,1,0:T(8,128)(2,1)} %bitcast.34), calls=%async_computation.4 | async-start | bytes 1572864 | tf_op jit(solution)/shard_map/all_to_all | solution.py:265
  137.5 21.0 %collective-permute-start.1 = (bf16[768,384]{1,0:T(8,128)(2,1)}, bf16[768,384]{1,0:T(8,128)(2,1)}, u32[]{:S(2)}, u32[]{:S(2)}) collective-permute-start(bf16[768,384]{1,0:T(8,128)(2,1)} %convolution_convert_fusion.2), channel_id=1, source_target_pairs={{0,16},{16,0},{1,17},{17,1},{2,18},{18,2},{3,19},{19,3},{4,20},{20... | collective-permute-start | bytes 1769480 | tf_op jit(solution)/shard_map/ppermute | solution.py:277
  150.2 13.4 %all-to-all-start.5 = ((bf16[4,128,768]{2,1,0:T(8,128)(2,1)}), bf16[4,128,768]{2,1,0:T(8,128)(2,1)S(1)}, u32[]{:S(2)}, u32[]{:S(2)}) async-start(bf16[4,128,768]{2,1,0:T(8,128)(2,1)} %broadcast_in_dim.33), calls=%async_computation.5 | async-start | bytes 1572864 | tf_op jit(solution)/shard_map/all_to_all | solution.py:265
  153.7 60.9 %reduce-scatter.6.cloned.1.call-start = ((), (), s32[]{:S(2)}) async-start(), calls=%async_computation.15 | async-start | bytes 1658880 | tf_op jit(solution)/shard_map/reduce_scatter | solution.py:402
  156.4 11.1 %collective-permute-start = (bf16[768,384]{1,0:T(8,128)(2,1)}, bf16[768,384]{1,0:T(8,128)(2,1)}, u32[]{:S(2)}, u32[]{:S(2)}) collective-permute-start(bf16[768,384]{1,0:T(8,128)(2,1)} %convolution_convert_fusion.3), channel_id=1, source_target_pairs={{0,16},{16,0},{1,17},{17,1},{2,18},{18,2},{3,19},{19,3},{4,20},{20... | collective-permute-start | bytes 1769480 | tf_op jit(solution)/shard_map/ppermute | solution.py:277
  163.9 5.7 %collective-permute-start.2 = (bf16[192,384]{1,0:T(8,128)(2,1)S(1)}, bf16[192,384]{1,0:T(8,128)(2,1)S(1)}, u32[]{:S(2)}, u32[]{:S(2)}) collective-permute-start(bf16[192,384]{1,0:T(8,128)(2,1)S(1)} %convolution_convert_fusion.5), channel_id=1, source_target_pairs={{0,16},{16,0},{1,17},{17,1},{2,18},{18,2},{3,19},{19,3},{4,20},{20... | collective-permute-start | bytes 442376 | tf_op jit(solution)/shard_map/ppermute | solution.py:277
  182.6 27.6 %all-to-all-start.6 = ((bf16[4,512,384]{2,1,0:T(8,128)(2,1)}), bf16[4,512,384]{2,1,0:T(8,128)(2,1)}, u32[]{:S(2)}, u32[]{:S(2)}) async-start(bf16[4,512,384]{2,1,0:T(8,128)(2,1)} %get-tuple-element.35), calls=%async_computation.6 | async-start | bytes 3145728 | tf_op jit(solution)/shard_map/all_to_all | solution.py:265
  187.1 65.6 %reduce-scatter.8.cloned.1.call-start = ((), (), s32[]{:S(2)}) async-start(), calls=%async_computation.16 | async-start | bytes 245760 | tf_op jit(solution)/shard_map/reduce_scatter | solution.py:404
  192.5 19.7 %copy-start.4 = (bf16[4,224,768]{2,1,0:T(8,128)(2,1)S(1)}, bf16[4,224,768]{2,1,0:T(8,128)(2,1)}, u32[]{:S(2)}) copy-start(bf16[4,224,768]{2,1,0:T(8,128)(2,1)} %copy-done.3) | copy-start | bytes 4128772
  192.5 19.7 %copy-start.9 = (bf16[4,4,48,640]{3,2,0,1:T(8,128)(2,1)S(1)}, bf16[4,4,48,640]{3,2,0,1:T(8,128)(2,1)}, u32[]{:S(2)}) copy-start(bf16[4,4,48,640]{3,2,0,1:T(8,128)(2,1)} %copy-done.8) | copy-start | bytes 2949124
  193.3 18.9 %copy-start.16 = (bf16[512,192]{0,1:T(8,128)(2,1)S(1)}, bf16[512,192]{0,1:T(8,128)(2,1)}, u32[]{:S(2)}) copy-start(bf16[512,192]{0,1:T(8,128)(2,1)} %copy.126) | copy-start | bytes 589828
  193.3 18.9 %copy-start.28 = (f32[512]{0:T(512)S(1)}, f32[512]{0:T(512)}, u32[]{:S(2)}) copy-start(f32[512]{0:T(512)} %get-tuple-element.86) | copy-start | bytes 6148
  193.3 18.9 %copy-start.29 = (f32[512]{0:T(512)S(1)}, f32[512]{0:T(512)}, u32[]{:S(2)}) copy-start(f32[512]{0:T(512)} %get-tuple-element.88) | copy-start | bytes 6148
  216.3 53.4 %reduce-scatter.4.cloned.1.call-start = ((), (), s32[]{:S(2)}) async-start(), calls=%async_computation.14 | async-start | bytes 1966080 | tf_op jit(solution)/shard_map/reduce_scatter | solution.py:413
  223.1 2.5 collective-permute-start.3
  262.8 5.6 %collective-permute-start.4 = (bf16[4,160,384]{2,1,0:T(8,128)(2,1)S(1)}, bf16[4,160,384]{2,1,0:T(8,128)(2,1)S(1)}, u32[]{:S(2)}, u32[]{:S(2)}) collective-permute-start(bf16[4,160,384]{2,1,0:T(8,128)(2,1)S(1)} %all_to_all.52.mine_ref), channel_id=1, source_target_pairs={{0,16},{16,0},{1,17},{17,1},{2,18},{18,2},{3,19},{19,3},{4,20},{20... | collective-permute-start | bytes 1474568 | tf_op jit(solution)/shard_map/ppermute | solution.py:277
  (26 other events, 105.7 us)
Sparse Core Ops, SparseCore 0:
  10.2 28.8 all-gather.7
  46.7 25.2 all-gather.5
  74.2 38.4 all-gather.9
  171.3 23.9 reduce-scatter.5
  216.4 18.5 reduce-scatter.7
  237.4 29.6 reduce-scatter.3
